TPU v7x, 32 devices: a whole 2x2x4 slice. The times are simulated.
32 devices in a mesh: seq: 4 (over y, x), head: 8 (over z, core).
Axes of the slice: x: 2, y: 2, z: 4, core: 2. Of those that a mesh axis runs over, the one named last changes fastest.
Arguments:
- q_raw: bfloat16 [1536, 1024], P('seq', 'head'), may hold values from -300 to 300
- k_raw: bfloat16 [1536, 1024], P('seq', 'head'), may hold values from -300 to 300
- values: bfloat16 [1536, 1024], P('seq', 'head'), may hold values from -6 to 6
- out: bfloat16 [1536, 1024], P('seq', 'head'), may hold values from -6 to 6
- d_out: bfloat16 [1536, 1024], P('seq', 'head'), may hold values from -6 to 6
- q_gain: bfloat16 [1024], P('head'), may hold values from 0.25 to 1.75
- k_gain: bfloat16 [1024], P('head'), may hold values from 0.25 to 1.75
- order: int32 [4], replicated, may hold values from 0 to 3, each once
Outputs:
- d_q: bfloat16 [1536, 1024], P('seq', 'head')
- d_k: bfloat16 [1536, 1024], P('seq', 'head')
- d_v: bfloat16 [1536, 1024], P('seq', 'head')
All inputs are finite; a program needn't handle non-finite values.
Results may differ from a plain program's by a relative error of at most 0.025.
Values may be sent and summed in bfloat16 or wider, within the bound.
A program may use at most 64 MiB of HBM per device.

v0:
```python
import jax
import jax.numpy as jnp
from jax import lax
from jax.sharding import PartitionSpec as P

EPSILON = 1e-06


def from_behind(value, axis, steps):
    count = lax.axis_size(axis)
    pairs = [(source, (source + steps) % count) for source in range(count)]
    return lax.ppermute(value, axis, pairs)


def lookup(table, index):
    return jnp.sum(jnp.where(jnp.arange(table.shape[0], dtype=jnp.int32) == index, table, 0))


def rounded(partial_value):
    return lax.optimization_barrier(partial_value.astype(jnp.bfloat16)).astype(jnp.float32)


def block_total(queries, keys, visible):
    reciprocal_root = keys.shape[1] ** (-0.5)

    def compute():
        scores = jnp.dot(queries, keys.T, preferred_element_type=jnp.float32) * reciprocal_root
        return jnp.sum(jnp.exp(scores), axis=1)

    return compute() * visible.astype(jnp.float32)


def block_grads(queries, grad_out, log_total, delta, keys, vals, visible):
    reciprocal_root = keys.shape[1] ** (-0.5)
    contract = (((0,), (0,)), ((), ()))

    def compute(weight):
        scores = jnp.dot(queries, keys.T, preferred_element_type=jnp.float32) * reciprocal_root
        probs = jnp.exp(scores - log_total[:, None]) * weight
        probs_low = probs.astype(jnp.bfloat16)
        dprobs = jnp.dot(grad_out, vals.T, preferred_element_type=jnp.float32)
        dscores = (probs * (dprobs - delta[:, None])).astype(jnp.bfloat16)
        query_add = jnp.dot(dscores, keys, preferred_element_type=jnp.float32) * reciprocal_root
        key_add = (
            lax.dot_general(dscores, queries, contract, preferred_element_type=jnp.float32)
            * reciprocal_root
        )
        value_add = lax.dot_general(
            probs_low, grad_out, contract, preferred_element_type=jnp.float32
        )
        return (query_add, key_add, value_add)

    return compute(visible.astype(jnp.float32))


def local(q_raw, k_raw, values, out, d_out, q_gain, k_gain, order):
    device = lax.axis_index("seq")
    cycle_size = lax.axis_size("seq")
    feature_count = lax.axis_size("head") * q_raw.shape[1]
    rows_here = q_raw.shape[0]
    head_width = q_raw.shape[1]
    q_float = q_raw.astype(jnp.float32)
    k_float = k_raw.astype(jnp.float32)
    squares = lax.psum(
        (jnp.sum(q_float * q_float, axis=1), jnp.sum(k_float * k_float, axis=1)), "head"
    )
    q_rate = lax.rsqrt(squares[0] / feature_count + EPSILON)
    k_rate = lax.rsqrt(squares[1] / feature_count + EPSILON)
    q_scale = q_gain.astype(jnp.float32)
    k_scale = k_gain.astype(jnp.float32)
    q_norm = (q_float * q_rate[:, None] * q_scale).astype(jnp.bfloat16)
    k_norm = (k_float * k_rate[:, None] * k_scale).astype(jnp.bfloat16)
    own_group = lookup(order, device)
    delta = jnp.sum(d_out.astype(jnp.float32) * out.astype(jnp.float32), axis=1)
    last_source = (device + 1) % cycle_size
    zeros_block = jnp.zeros((rows_here, head_width), jnp.float32)

    def stat_turn(turn, state_tuple):
        held_keys, row_total = state_tuple
        source = (device - turn + cycle_size) % cycle_size
        row_total = row_total + block_total(q_norm, held_keys, lookup(order, source) <= own_group)
        held_keys = from_behind(held_keys, "seq", 1)
        return (held_keys, row_total)

    held_keys, row_total = lax.fori_loop(
        0, cycle_size - 1, stat_turn, (k_norm, jnp.zeros((rows_here,), jnp.float32))
    )
    row_total = row_total + block_total(q_norm, held_keys, lookup(order, last_source) <= own_group)
    log_total = jnp.log(row_total)

    def key_update(state_tuple, source):
        key_block, value_block, key_sums, value_sums, query_sum = state_tuple
        visible = lookup(order, source) <= own_group
        query_add, key_add, value_add = block_grads(
            q_norm, d_out, log_total, delta, key_block, value_block, visible
        )
        return (
            key_block,
            value_block,
            key_sums + rounded(key_add),
            value_sums + rounded(value_add),
            query_sum + query_add,
        )

    def key_turn(turn, state_tuple):
        state_tuple = key_update(state_tuple, (device - turn + cycle_size) % cycle_size)
        key_block, value_block = from_behind((state_tuple[0], state_tuple[1]), "seq", 1)
        key_sums, value_sums = (
            from_behind(state_tuple[2].astype(jnp.bfloat16), "seq", 1).astype(jnp.float32),
            from_behind(state_tuple[3].astype(jnp.bfloat16), "seq", 1).astype(jnp.float32),
        )
        return (key_block, value_block, key_sums, value_sums, state_tuple[4])

    final_state = lax.fori_loop(
        0, cycle_size - 1, key_turn, (k_norm, values, zeros_block, zeros_block, zeros_block)
    )
    final_state = key_update(final_state, last_source)
    key_grad, value_grad = (
        from_behind(final_state[2].astype(jnp.bfloat16), "seq", 1).astype(jnp.float32),
        from_behind(final_state[3].astype(jnp.bfloat16), "seq", 1).astype(jnp.float32),
    )
    query_grad = final_state[4]
    q_grad = query_grad * q_scale
    k_grad = key_grad * k_scale
    inner = lax.psum((jnp.sum(q_grad * q_float, axis=1), jnp.sum(k_grad * k_float, axis=1)), "head")
    d_q = q_rate[:, None] * q_grad - q_float * (q_rate**3 * inner[0] / feature_count)[:, None]
    d_k = k_rate[:, None] * k_grad - k_float * (k_rate**3 * inner[1] / feature_count)[:, None]
    return (d_q.astype(jnp.bfloat16), d_k.astype(jnp.bfloat16), value_grad.astype(jnp.bfloat16))


def solution(mesh):
    in_specs = (
        P("seq", "head"),
        P("seq", "head"),
        P("seq", "head"),
        P("seq", "head"),
        P("seq", "head"),
        P("head"),
        P("head"),
        P(),
    )
    out_specs = (P("seq", "head"), P("seq", "head"), P("seq", "head"))
    return jax.shard_map(local, mesh=mesh, in_specs=in_specs, out_specs=out_specs, check_vma=False)
```

profile of v0, /device:TPU:0, one launch (start us, length us, event | category | flops | bytes accessed | tf_op | source)
XLA Modules:
  0.0 106.3 jit_solution(15473899991052886260)
XLA Ops:
  0.7 0.8 copy-done.2
  1.7 0.8 copy-done.3
  2.7 18.1 %all-reduce.1 = (f32[384]{0:T(512)S(1)}, f32[384]{0:T(512)S(1)}) all-reduce(f32[384]{0:T(512)S(1)} %fusion.32, f32[384]{0:T(512)S(1)} %fusion.26), channel_id=1, replica_groups=mesh['seq'=4,'head'=8] {'head'}, use_global_device_ids=true, to_apply=%region_3.0 | all-reduce | flops 768 | bytes 6144 | tf_op jit(solution)/shard_map/psum | solution.py:64
  20.8 0.6 copy-done.6
  21.7 0.6 copy-done.7
  22.6 0.6 copy-done.5
  23.2 0.7 fusion.43
  23.9 17.9 %while.42 = (s32[]{:T(128)}, bf16[384,128]{1,0:T(8,128)(2,1)S(1)}, f32[384]{0:T(512)S(1)}, bf16[384,128]{1,0:T(8,128)(2,1)S(1)}, s32[]{:T(128)}, /*index=5*/s32[...) while((s32[]{:T(128)}, bf16[384,128]{1,0:T(8,128)(2,1)S(1)}, ...), condition=%wide.region_8.9_spmd.clone, body=%wide.region_5.8_spmd.clone.sunk | while | flops 38044428 | bytes 792910 | solution.py:85
  24.0 1.5 %collective-permute-start = (bf16[384,128]{1,0:T(8,128)(2,1)S(1)}, bf16[384,128]{1,0:T(8,128)(2,1)S(1)}, u32[]{:S(2)}, u32[]{:S(2)}) collective-permute-start(bf16[384,128]{1,0:T(8,128)(2,1)S(1)} %copy.29), channel_id=1, source_target_pairs={{0,8},{8,16},{16,24},{24,0},{1,9},{9,17},{17,25},{25,1},{2,10},{10... | collective-permute-start | bytes 294920 | tf_op jit(solution)/shard_map/while/body/eval_jaxpr/ppermute | solution.py:12
  25.5 0.7 fusion.90
  27.4 0.3 fusion.89
  27.7 2.5 %collective-permute-done = bf16[384,128]{1,0:T(8,128)(2,1)S(1)} collective-permute-done((bf16[384,128]{1,0:T(8,128)(2,1)S(1)}, bf16[384,128]{1,0:T(8,128)(2,1)S(1)}, u32[]{:S(2)}, u32[]{:S(2)}) %collective-permute-start) | collective-permute-done | bytes 98336 | tf_op jit(solution)/shard_map/while/body/eval_jaxpr/ppermute | solution.py:12
  30.2 0.6 collective-permute-start
  30.8 0.7 fusion.90
  32.7 0.3 fusion.89
  33.0 3.1 %collective-permute-done = bf16[384,128]{1,0:T(8,128)(2,1)S(1)} collective-permute-done((bf16[384,128]{1,0:T(8,128)(2,1)S(1)}, bf16[384,128]{1,0:T(8,128)(2,1)S(1)}, u32[]{:S(2)}, u32[]{:S(2)}) %collective-permute-start) | collective-permute-done | bytes 98336 | tf_op jit(solution)/shard_map/while/body/eval_jaxpr/ppermute | solution.py:12
  36.2 0.7 fusion.90
  38.0 0.3 fusion.89
  38.3 3.5 %collective-permute-done = bf16[384,128]{1,0:T(8,128)(2,1)S(1)} collective-permute-done((bf16[384,128]{1,0:T(8,128)(2,1)S(1)}, bf16[384,128]{1,0:T(8,128)(2,1)S(1)}, u32[]{:S(2)}, u32[]{:S(2)}) %collective-permute-start) | collective-permute-done | bytes 98336 | tf_op jit(solution)/shard_map/while/body/eval_jaxpr/ppermute | solution.py:12
  43.5 0.7 copy-done.1
  44.3 37.8 %while.43 = (s32[]{:T(128)}, bf16[384,128]{1,0:T(8,128)(2,1)S(1)}, bf16[384,128]{1,0:T(8,128)(2,1)S(1)}, f32[384,128]{1,0:T(8,128)S(1)}, f32[384,128]{1,0:T(8,12...) while((s32[]{:T(128)}, bf16[384,128]{1,0:T(8,128)(2,1)S(1)}, ...), condition=%wide.region_14.15_spmd.clone, body=%wide.region_12.14_spmd.clone.sunk | while | flops 190562336 | bytes 7278072 | solution.py:114
  44.4 3.0 %collective-permute-start.2 = (bf16[384,128]{1,0:T(8,128)(2,1)S(1)}, bf16[384,128]{1,0:T(8,128)(2,1)S(1)}, u32[]{:S(2)}, u32[]{:S(2)}) collective-permute-start(bf16[384,128]{1,0:T(8,128)(2,1)S(1)} %copy.42), channel_id=1, source_target_pairs={{0,8},{8,16},{16,24},{24,0},{1,9},{9,17},{17,25},{25,1},{2,10},{10... | collective-permute-start | bytes 294920 | tf_op jit(solution)/shard_map/while/body/eval_jaxpr/ppermute | solution.py:12
  47.4 0.6 fusion.101
  50.2 0.3 convolution_convert_fusion.3
  50.5 2.0 %collective-permute-start.4 = (bf16[384,128]{1,0:T(8,128)(2,1)S(1)}, bf16[384,128]{1,0:T(8,128)(2,1)S(1)}, u32[]{:S(2)}, u32[]{:S(2)}) collective-permute-start(bf16[384,128]{1,0:T(8,128)(2,1)S(1)} %fusion.106), channel_id=1, source_target_pairs={{0,8},{8,16},{16,24},{24,0},{1,9},{9,17},{17,25},{25,1},{2,10},{10... | collective-permute-start | bytes 294920 | tf_op jit(solution)/shard_map/while/body/eval_jaxpr/ppermute | solution.py:12
  52.5 0.3 fusion.107
  52.8 2.9 %collective-permute-done.3 = bf16[384,128]{1,0:T(8,128)(2,1)S(1)} collective-permute-done((bf16[384,128]{1,0:T(8,128)(2,1)S(1)}, bf16[384,128]{1,0:T(8,128)(2,1)S(1)}, u32[]{:S(2)}, u32[]{:S(2)}) %collective-permute-start.3) | collective-permute-done | bytes 98336 | tf_op jit(solution)/shard_map/while/body/eval_jaxpr/ppermute | solution.py:12
  55.7 1.2 %collective-permute-done.4 = bf16[384,128]{1,0:T(8,128)(2,1)S(1)} collective-permute-done((bf16[384,128]{1,0:T(8,128)(2,1)S(1)}, bf16[384,128]{1,0:T(8,128)(2,1)S(1)}, u32[]{:S(2)}, u32[]{:S(2)}) %collective-permute-start.4) | collective-permute-done | bytes 98336 | tf_op jit(solution)/shard_map/while/body/eval_jaxpr/ppermute | solution.py:12
  57.2 2.5 %collective-permute-start.2 = (bf16[384,128]{1,0:T(8,128)(2,1)S(1)}, bf16[384,128]{1,0:T(8,128)(2,1)S(1)}, u32[]{:S(2)}, u32[]{:S(2)}) collective-permute-start(bf16[384,128]{1,0:T(8,128)(2,1)S(1)} %copy.42), channel_id=1, source_target_pairs={{0,8},{8,16},{16,24},{24,0},{1,9},{9,17},{17,25},{25,1},{2,10},{10... | collective-permute-start | bytes 294920 | tf_op jit(solution)/shard_map/while/body/eval_jaxpr/ppermute | solution.py:12
  59.8 0.6 fusion.101
  62.5 0.7 collective-permute-start.3
  63.5 1.7 %collective-permute-start.4 = (bf16[384,128]{1,0:T(8,128)(2,1)S(1)}, bf16[384,128]{1,0:T(8,128)(2,1)S(1)}, u32[]{:S(2)}, u32[]{:S(2)}) collective-permute-start(bf16[384,128]{1,0:T(8,128)(2,1)S(1)} %fusion.106), channel_id=1, source_target_pairs={{0,8},{8,16},{16,24},{24,0},{1,9},{9,17},{17,25},{25,1},{2,10},{10... | collective-permute-start | bytes 294920 | tf_op jit(solution)/shard_map/while/body/eval_jaxpr/ppermute | solution.py:12
  65.5 3.0 %collective-permute-done.3 = bf16[384,128]{1,0:T(8,128)(2,1)S(1)} collective-permute-done((bf16[384,128]{1,0:T(8,128)(2,1)S(1)}, bf16[384,128]{1,0:T(8,128)(2,1)S(1)}, u32[]{:S(2)}, u32[]{:S(2)}) %collective-permute-start.3) | collective-permute-done | bytes 98336 | tf_op jit(solution)/shard_map/while/body/eval_jaxpr/ppermute | solution.py:12
  68.5 2.1 %collective-permute-done.4 = bf16[384,128]{1,0:T(8,128)(2,1)S(1)} collective-permute-done((bf16[384,128]{1,0:T(8,128)(2,1)S(1)}, bf16[384,128]{1,0:T(8,128)(2,1)S(1)}, u32[]{:S(2)}, u32[]{:S(2)}) %collective-permute-start.4) | collective-permute-done | bytes 98336 | tf_op jit(solution)/shard_map/while/body/eval_jaxpr/ppermute | solution.py:12
  70.7 1.4 %collective-permute-start.2 = (bf16[384,128]{1,0:T(8,128)(2,1)S(1)}, bf16[384,128]{1,0:T(8,128)(2,1)S(1)}, u32[]{:S(2)}, u32[]{:S(2)}) collective-permute-start(bf16[384,128]{1,0:T(8,128)(2,1)S(1)} %copy.42), channel_id=1, source_target_pairs={{0,8},{8,16},{16,24},{24,0},{1,9},{9,17},{17,25},{25,1},{2,10},{10... | collective-permute-start | bytes 294920 | tf_op jit(solution)/shard_map/while/body/eval_jaxpr/ppermute | solution.py:12
  72.1 0.6 fusion.101
  74.9 1.3 %collective-permute-start.3 = (bf16[384,128]{1,0:T(8,128)(2,1)S(1)}, bf16[384,128]{1,0:T(8,128)(2,1)S(1)}, u32[]{:S(2)}, u32[]{:S(2)}) collective-permute-start(bf16[384,128]{1,0:T(8,128)(2,1)S(1)} %fusion.105), channel_id=1, source_target_pairs={{0,8},{8,16},{16,24},{24,0},{1,9},{9,17},{17,25},{25,1},{2,10},{10... | collective-permute-start | bytes 294920 | tf_op jit(solution)/shard_map/while/body/eval_jaxpr/ppermute | solution.py:12
  76.5 2.4 %collective-permute-start.4 = (bf16[384,128]{1,0:T(8,128)(2,1)S(1)}, bf16[384,128]{1,0:T(8,128)(2,1)S(1)}, u32[]{:S(2)}, u32[]{:S(2)}) collective-permute-start(bf16[384,128]{1,0:T(8,128)(2,1)S(1)} %fusion.106), channel_id=1, source_target_pairs={{0,8},{8,16},{16,24},{24,0},{1,9},{9,17},{17,25},{25,1},{2,10},{10... | collective-permute-start | bytes 294920 | tf_op jit(solution)/shard_map/while/body/eval_jaxpr/ppermute | solution.py:12
  79.1 1.3 %collective-permute-done.3 = bf16[384,128]{1,0:T(8,128)(2,1)S(1)} collective-permute-done((bf16[384,128]{1,0:T(8,128)(2,1)S(1)}, bf16[384,128]{1,0:T(8,128)(2,1)S(1)}, u32[]{:S(2)}, u32[]{:S(2)}) %collective-permute-start.3) | collective-permute-done | bytes 98336 | tf_op jit(solution)/shard_map/while/body/eval_jaxpr/ppermute | solution.py:12
  80.5 1.6 %collective-permute-done.4 = bf16[384,128]{1,0:T(8,128)(2,1)S(1)} collective-permute-done((bf16[384,128]{1,0:T(8,128)(2,1)S(1)}, bf16[384,128]{1,0:T(8,128)(2,1)S(1)}, u32[]{:S(2)}, u32[]{:S(2)}) %collective-permute-start.4) | collective-permute-done | bytes 98336 | tf_op jit(solution)/shard_map/while/body/eval_jaxpr/ppermute | solution.py:12
  82.6 1.5 %collective-permute-start.6 = (bf16[384,128]{1,0:T(8,128)(2,1)S(1)}, bf16[384,128]{1,0:T(8,128)(2,1)S(1)}, u32[]{:S(2)}, u32[]{:S(2)}) collective-permute-start(bf16[384,128]{1,0:T(8,128)(2,1)S(1)} %add_convert_fusion), channel_id=1, source_target_pairs={{0,8},{8,16},{16,24},{24,0},{1,9},{9,17},{17,25},{25,1},{2,10},{10... | collective-permute-start | bytes 294920 | tf_op jit(solution)/shard_map/ppermute | solution.py:12
  84.8 1.6 %collective-permute-start.5 = (bf16[384,128]{0,1:T(8,128)(2,1)S(1)}, bf16[384,128]{0,1:T(8,128)(2,1)S(1)}, u32[]{:S(2)}, u32[]{:S(2)}) collective-permute-start(bf16[384,128]{0,1:T(8,128)(2,1)S(1)} %add_convert_fusion.1), channel_id=1, source_target_pairs={{0,8},{8,16},{16,24},{24,0},{1,9},{9,17},{17,25},{25,1},{2,10},{10... | collective-permute-start | bytes 294920 | tf_op jit(solution)/shard_map/ppermute | solution.py:12
  86.5 0.3 fusion.29
  86.8 3.5 %collective-permute-done.5 = bf16[384,128]{0,1:T(8,128)(2,1)S(1)} collective-permute-done((bf16[384,128]{0,1:T(8,128)(2,1)S(1)}, bf16[384,128]{0,1:T(8,128)(2,1)S(1)}, u32[]{:S(2)}, u32[]{:S(2)}) %collective-permute-start.5) | collective-permute-done | bytes 98336 | tf_op jit(solution)/shard_map/ppermute | solution.py:12
  90.4 13.6 %all-reduce = (f32[384]{0:T(512)S(1)}, f32[384]{0:T(512)S(1)}) all-reduce(f32[384]{0:T(512)S(1)} %get-tuple-element.636, f32[384]{0:T(512)S(1)} %fusion.35), channel_id=1, replica_groups=mesh['seq'=4,'head'=8] {'head'}, use_global_device_ids=true, to_apply=%region_16.17 | all-reduce | flops 768 | bytes 6144 | tf_op jit(solution)/shard_map/psum | solution.py:125
  104.2 0.8 copy.22
  104.9 0.8 copy.21
  105.7 0.6 copy.55
  (91 shorter events, 7.3 us)
Async XLA Ops:
  0.6 0.9 copy-start.2
  1.6 0.9 copy-start.3
  20.8 0.7 copy-start.6
  21.7 0.7 copy-start.7
  22.6 0.7 copy-start.5
  24.0 6.2 %collective-permute-start = (bf16[384,128]{1,0:T(8,128)(2,1)S(1)}, bf16[384,128]{1,0:T(8,128)(2,1)S(1)}, u32[]{:S(2)}, u32[]{:S(2)}) collective-permute-start(bf16[384,128]{1,0:T(8,128)(2,1)S(1)} %copy.29), channel_id=1, source_target_pairs={{0,8},{8,16},{16,24},{24,0},{1,9},{9,17},{17,25},{25,1},{2,10},{10... | collective-permute-start | bytes 294920 | tf_op jit(solution)/shard_map/while/body/eval_jaxpr/ppermute | solution.py:12
  30.2 5.9 %collective-permute-start = (bf16[384,128]{1,0:T(8,128)(2,1)S(1)}, bf16[384,128]{1,0:T(8,128)(2,1)S(1)}, u32[]{:S(2)}, u32[]{:S(2)}) collective-permute-start(bf16[384,128]{1,0:T(8,128)(2,1)S(1)} %copy.29), channel_id=1, source_target_pairs={{0,8},{8,16},{16,24},{24,0},{1,9},{9,17},{17,25},{25,1},{2,10},{10... | collective-permute-start | bytes 294920 | tf_op jit(solution)/shard_map/while/body/eval_jaxpr/ppermute | solution.py:12
  36.1 5.8 %collective-permute-start = (bf16[384,128]{1,0:T(8,128)(2,1)S(1)}, bf16[384,128]{1,0:T(8,128)(2,1)S(1)}, u32[]{:S(2)}, u32[]{:S(2)}) collective-permute-start(bf16[384,128]{1,0:T(8,128)(2,1)S(1)} %copy.29), channel_id=1, source_target_pairs={{0,8},{8,16},{16,24},{24,0},{1,9},{9,17},{17,25},{25,1},{2,10},{10... | collective-permute-start | bytes 294920 | tf_op jit(solution)/shard_map/while/body/eval_jaxpr/ppermute | solution.py:12
  41.8 1.5 %copy-start = (bf16[384,128]{1,0:T(8,128)(2,1)S(1)}, bf16[384,128]{1,0:T(8,128)(2,1)}, u32[]{:S(2)}) copy-start(bf16[384,128]{1,0:T(8,128)(2,1)} %param.16) | copy-start | bytes 294916
  41.8 1.5 %copy-start.4 = (bf16[384,128]{1,0:T(8,128)(2,1)S(1)}, bf16[384,128]{1,0:T(8,128)(2,1)}, u32[]{:S(2)}) copy-start(bf16[384,128]{1,0:T(8,128)(2,1)} %param.15) | copy-start | bytes 294916
  43.4 0.9 copy-start.1
  44.3 12.6 %collective-permute-start.1 = (bf16[384,128]{1,0:T(8,128)(2,1)S(1)}, bf16[384,128]{1,0:T(8,128)(2,1)S(1)}, u32[]{:S(2)}, u32[]{:S(2)}) collective-permute-start(bf16[384,128]{1,0:T(8,128)(2,1)S(1)} %copy.41), channel_id=1, source_target_pairs={{0,8},{8,16},{16,24},{24,0},{1,9},{9,17},{17,25},{25,1},{2,10},{10... | collective-permute-start | bytes 294920 | tf_op jit(solution)/shard_map/while/body/eval_jaxpr/ppermute | solution.py:12
  44.4 12.6 %collective-permute-start.2 = (bf16[384,128]{1,0:T(8,128)(2,1)S(1)}, bf16[384,128]{1,0:T(8,128)(2,1)S(1)}, u32[]{:S(2)}, u32[]{:S(2)}) collective-permute-start(bf16[384,128]{1,0:T(8,128)(2,1)S(1)} %copy.42), channel_id=1, source_target_pairs={{0,8},{8,16},{16,24},{24,0},{1,9},{9,17},{17,25},{25,1},{2,10},{10... | collective-permute-start | bytes 294920 | tf_op jit(solution)/shard_map/while/body/eval_jaxpr/ppermute | solution.py:12
  50.1 5.6 %collective-permute-start.3 = (bf16[384,128]{1,0:T(8,128)(2,1)S(1)}, bf16[384,128]{1,0:T(8,128)(2,1)S(1)}, u32[]{:S(2)}, u32[]{:S(2)}) collective-permute-start(bf16[384,128]{1,0:T(8,128)(2,1)S(1)} %fusion.105), channel_id=1, source_target_pairs={{0,8},{8,16},{16,24},{24,0},{1,9},{9,17},{17,25},{25,1},{2,10},{10... | collective-permute-start | bytes 294920 | tf_op jit(solution)/shard_map/while/body/eval_jaxpr/ppermute | solution.py:12
  50.5 6.4 %collective-permute-start.4 = (bf16[384,128]{1,0:T(8,128)(2,1)S(1)}, bf16[384,128]{1,0:T(8,128)(2,1)S(1)}, u32[]{:S(2)}, u32[]{:S(2)}) collective-permute-start(bf16[384,128]{1,0:T(8,128)(2,1)S(1)} %fusion.106), channel_id=1, source_target_pairs={{0,8},{8,16},{16,24},{24,0},{1,9},{9,17},{17,25},{25,1},{2,10},{10... | collective-permute-start | bytes 294920 | tf_op jit(solution)/shard_map/while/body/eval_jaxpr/ppermute | solution.py:12
  57.0 13.6 %collective-permute-start.1 = (bf16[384,128]{1,0:T(8,128)(2,1)S(1)}, bf16[384,128]{1,0:T(8,128)(2,1)S(1)}, u32[]{:S(2)}, u32[]{:S(2)}) collective-permute-start(bf16[384,128]{1,0:T(8,128)(2,1)S(1)} %copy.41), channel_id=1, source_target_pairs={{0,8},{8,16},{16,24},{24,0},{1,9},{9,17},{17,25},{25,1},{2,10},{10... | collective-permute-start | bytes 294920 | tf_op jit(solution)/shard_map/while/body/eval_jaxpr/ppermute | solution.py:12
  57.2 13.4 %collective-permute-start.2 = (bf16[384,128]{1,0:T(8,128)(2,1)S(1)}, bf16[384,128]{1,0:T(8,128)(2,1)S(1)}, u32[]{:S(2)}, u32[]{:S(2)}) collective-permute-start(bf16[384,128]{1,0:T(8,128)(2,1)S(1)} %copy.42), channel_id=1, source_target_pairs={{0,8},{8,16},{16,24},{24,0},{1,9},{9,17},{17,25},{25,1},{2,10},{10... | collective-permute-start | bytes 294920 | tf_op jit(solution)/shard_map/while/body/eval_jaxpr/ppermute | solution.py:12
  62.5 6.0 %collective-permute-start.3 = (bf16[384,128]{1,0:T(8,128)(2,1)S(1)}, bf16[384,128]{1,0:T(8,128)(2,1)S(1)}, u32[]{:S(2)}, u32[]{:S(2)}) collective-permute-start(bf16[384,128]{1,0:T(8,128)(2,1)S(1)} %fusion.105), channel_id=1, source_target_pairs={{0,8},{8,16},{16,24},{24,0},{1,9},{9,17},{17,25},{25,1},{2,10},{10... | collective-permute-start | bytes 294920 | tf_op jit(solution)/shard_map/while/body/eval_jaxpr/ppermute | solution.py:12
  63.5 7.1 %collective-permute-start.4 = (bf16[384,128]{1,0:T(8,128)(2,1)S(1)}, bf16[384,128]{1,0:T(8,128)(2,1)S(1)}, u32[]{:S(2)}, u32[]{:S(2)}) collective-permute-start(bf16[384,128]{1,0:T(8,128)(2,1)S(1)} %fusion.106), channel_id=1, source_target_pairs={{0,8},{8,16},{16,24},{24,0},{1,9},{9,17},{17,25},{25,1},{2,10},{10... | collective-permute-start | bytes 294920 | tf_op jit(solution)/shard_map/while/body/eval_jaxpr/ppermute | solution.py:12
  70.6 11.4 %collective-permute-start.1 = (bf16[384,128]{1,0:T(8,128)(2,1)S(1)}, bf16[384,128]{1,0:T(8,128)(2,1)S(1)}, u32[]{:S(2)}, u32[]{:S(2)}) collective-permute-start(bf16[384,128]{1,0:T(8,128)(2,1)S(1)} %copy.41), channel_id=1, source_target_pairs={{0,8},{8,16},{16,24},{24,0},{1,9},{9,17},{17,25},{25,1},{2,10},{10... | collective-permute-start | bytes 294920 | tf_op jit(solution)/shard_map/while/body/eval_jaxpr/ppermute | solution.py:12
  70.7 11.4 %collective-permute-start.2 = (bf16[384,128]{1,0:T(8,128)(2,1)S(1)}, bf16[384,128]{1,0:T(8,128)(2,1)S(1)}, u32[]{:S(2)}, u32[]{:S(2)}) collective-permute-start(bf16[384,128]{1,0:T(8,128)(2,1)S(1)} %copy.42), channel_id=1, source_target_pairs={{0,8},{8,16},{16,24},{24,0},{1,9},{9,17},{17,25},{25,1},{2,10},{10... | collective-permute-start | bytes 294920 | tf_op jit(solution)/shard_map/while/body/eval_jaxpr/ppermute | solution.py:12
  74.9 5.6 %collective-permute-start.3 = (bf16[384,128]{1,0:T(8,128)(2,1)S(1)}, bf16[384,128]{1,0:T(8,128)(2,1)S(1)}, u32[]{:S(2)}, u32[]{:S(2)}) collective-permute-start(bf16[384,128]{1,0:T(8,128)(2,1)S(1)} %fusion.105), channel_id=1, source_target_pairs={{0,8},{8,16},{16,24},{24,0},{1,9},{9,17},{17,25},{25,1},{2,10},{10... | collective-permute-start | bytes 294920 | tf_op jit(solution)/shard_map/while/body/eval_jaxpr/ppermute | solution.py:12
  76.5 5.6 %collective-permute-start.4 = (bf16[384,128]{1,0:T(8,128)(2,1)S(1)}, bf16[384,128]{1,0:T(8,128)(2,1)S(1)}, u32[]{:S(2)}, u32[]{:S(2)}) collective-permute-start(bf16[384,128]{1,0:T(8,128)(2,1)S(1)} %fusion.106), channel_id=1, source_target_pairs={{0,8},{8,16},{16,24},{24,0},{1,9},{9,17},{17,25},{25,1},{2,10},{10... | collective-permute-start | bytes 294920 | tf_op jit(solution)/shard_map/while/body/eval_jaxpr/ppermute | solution.py:12
  82.6 23.1 %collective-permute-start.6 = (bf16[384,128]{1,0:T(8,128)(2,1)S(1)}, bf16[384,128]{1,0:T(8,128)(2,1)S(1)}, u32[]{:S(2)}, u32[]{:S(2)}) collective-permute-start(bf16[384,128]{1,0:T(8,128)(2,1)S(1)} %add_convert_fusion), channel_id=1, source_target_pairs={{0,8},{8,16},{16,24},{24,0},{1,9},{9,17},{17,25},{25,1},{2,10},{10... | collective-permute-start | bytes 294920 | tf_op jit(solution)/shard_map/ppermute | solution.py:12
  84.8 5.6 %collective-permute-start.5 = (bf16[384,128]{0,1:T(8,128)(2,1)S(1)}, bf16[384,128]{0,1:T(8,128)(2,1)S(1)}, u32[]{:S(2)}, u32[]{:S(2)}) collective-permute-start(bf16[384,128]{0,1:T(8,128)(2,1)S(1)} %add_convert_fusion.1), channel_id=1, source_target_pairs={{0,8},{8,16},{16,24},{24,0},{1,9},{9,17},{17,25},{25,1},{2,10},{10... | collective-permute-start | bytes 294920 | tf_op jit(solution)/shard_map/ppermute | solution.py:12
where the time goes:
time: 107 us; the launch traced here: 106 us
  blocking collectives  31.7 us (30%)
  waiting for transfers between devices  24.7 us (23%)
  starting transfers between devices  20.7 us (19%)
  loops' own time  7.6 us (7%)
  local copies, waits for them, and re-layouts  7.32 us (7%)
  matrix products  6.5 us (6%)
  other arithmetic  5.65 us (5%)
  between operations  2.13 us (2%)
    ppermute x17, waiting for transfers between devices, from_behind(): return lax.ppermute(value, axis, pairs)  24.7 us
    ppermute x17, starting transfers between devices, from_behind(): return lax.ppermute(value, axis, pairs)  20.7 us
    psum x1, blocking collectives, local(): lax.psum((jnp.sum(q_float * q_float, axis=1), jnp.sum(k_float * k_float,...  18.1 us
    psum x1, blocking collectives, local(): lax.psum((jnp.sum(q_grad * q_float, axis=1), jnp.sum(k_grad * k_float, ax...  13.6 us
    unnamed x24, local copies, waits for them, and re-layouts  7 us
    reduce_sum x7, other arithmetic, lookup(): jnp.sum(jnp.where(jnp.arange(table.shape[0], dtype=jnp.int32) == index, t...  4.57 us
    another operation x1, loops' own time, local(): lax.fori_loop(0, cycle_size - 1, key_turn, (k_norm, values, zeros_block,...  3.92 us
    another operation x1, loops' own time, local(): lax.fori_loop(0, cycle_size - 1, stat_turn, (k_norm, jnp.zeros((rows_here...  3.67 us
  transfers between devices with their start and end apart: 17, of which 10 were waited for; matrix products, arithmetic and copies ran while one was open for 11% of the time, Pallas kernels for 0%

commit v1 on v0

v1 whole, which is shorter than its diff:
```python
import functools
import math

import jax
import jax.numpy as jnp
from jax import lax
from jax.experimental import pallas as pl
from jax.experimental.pallas import tpu as pltpu
from jax.sharding import PartitionSpec as P

EPSILON = 1e-06
HIDDEN = -1e30
MESH = pl.DeviceIdType.MESH
NN = (((1,), (0,)), ((), ()))
NT = (((1,), (1,)), ((), ()))


def dot(a, b, dims):
    return lax.dot_general(a, b, dims, preferred_element_type=jnp.float32)


def each(low, high, body):
    if high - low <= 8:
        for j in range(low, high):
            body(j)
    else:

        def step(j, carry):
            body(j)
            return carry

        lax.fori_loop(low, high, step, 0)


def kernel(
    n_s,
    n_h,
    order,
    q_raw,
    k_raw,
    values,
    out,
    d_out,
    q_gain,
    k_gain,
    d_q,
    d_k,
    d_v,
    x_t,
    y_t,
    qg_t,
    kg_t,
    keys,
    keys_t,
    exps,
    dscore,
    maxes,
    dk_sum,
    dv_sum,
    squares,
    grads,
    deltas,
    queries,
    stats,
    dq_out,
    dq_in,
    inner_q,
    inner_k,
    sq_send,
    sq_recv,
    gr_send,
    gr_recv,
    de_send,
    de_recv,
    qu_send,
    qu_recv,
    st_send,
    st_recv,
    dq_send,
    dq_recv,
    iq_send,
    iq_recv,
    ik_send,
    ik_recv,
):
    rows, width = q_raw.shape
    features = n_h * width
    root = width ** (-0.5)
    side = math.isqrt(n_s) if math.isqrt(n_s) ** 2 == n_s else n_s
    tall = n_s // side
    me = lax.axis_index("seq")
    mine = lax.axis_index("head")
    my_y, my_x = lax.div(me, side), lax.rem(me, side)

    def parts(j):
        if isinstance(j, int):
            return j // side, j % side
        return lax.div(j, side), lax.rem(j, side)

    def ahead(j):
        jy, jx = parts(j)
        return lax.rem(my_y + jy, tall) * side + lax.rem(my_x + jx, side)

    def behind(j):
        jy, jx = parts(j)
        return lax.rem(my_y + tall - jy, tall) * side + lax.rem(my_x + side - jx, side)

    def inverse(j):
        jy, jx = parts(j)
        if isinstance(j, int):
            return ((tall - jy) % tall) * side + (side - jx) % side
        return lax.rem(tall - jy, tall) * side + lax.rem(side - jx, side)

    def head_ahead(j):
        return lax.rem(mine + j, n_h)

    def seq_copy(src, dst, send, recv, j, peer):
        return pltpu.make_async_remote_copy(
            src_ref=src,
            dst_ref=dst.at[j],
            send_sem=send.at[j],
            recv_sem=recv.at[j],
            device_id=(peer, mine),
            device_id_type=MESH,
        )

    def head_copy(buffer, send, recv, j):
        return pltpu.make_async_remote_copy(
            src_ref=buffer.at[0],
            dst_ref=buffer.at[j],
            send_sem=send.at[j],
            recv_sem=recv.at[j],
            device_id=(me, head_ahead(j)),
            device_id_type=MESH,
        )

    barrier = pltpu.get_barrier_semaphore()

    def greet_seq(j):
        pl.semaphore_signal(barrier, inc=1, device_id=(ahead(j), mine), device_id_type=MESH)

    def greet_head(j):
        pl.semaphore_signal(barrier, inc=1, device_id=(me, head_ahead(j)), device_id_type=MESH)

    each(1, n_s, greet_seq)
    each(1, n_h, greet_head)

    x = q_raw[...].astype(jnp.float32).T
    y = k_raw[...].astype(jnp.float32).T
    x_t[...] = x
    y_t[...] = y
    squares[0, 0:1] = jnp.sum(x * x, axis=0, keepdims=True)
    squares[0, 1:2] = jnp.sum(y * y, axis=0, keepdims=True)
    grad = d_out[...].astype(jnp.float32)
    grads[0] = grad.T.astype(jnp.bfloat16)
    deltas[0] = jnp.sum((grad * out[...].astype(jnp.float32)).T, axis=0, keepdims=True)
    qg_t[...] = jnp.broadcast_to(q_gain[...].astype(jnp.float32), (rows, width)).T
    kg_t[...] = jnp.broadcast_to(k_gain[...].astype(jnp.float32), (rows, width)).T

    pl.semaphore_wait(barrier, n_s - 1 + n_h - 1)

    def squares_copy(j):
        return head_copy(squares, sq_send, sq_recv, j)

    def grads_copy(j):
        return seq_copy(grads.at[0], grads, gr_send, gr_recv, j, ahead(j))

    def deltas_copy(j):
        return seq_copy(deltas.at[0], deltas, de_send, de_recv, j, ahead(j))

    def queries_copy(j):
        return seq_copy(queries.at[0], queries, qu_send, qu_recv, j, ahead(j))

    def stats_copy(j):
        return seq_copy(stats.at[0], stats, st_send, st_recv, j, ahead(j))

    def dq_copy(j):
        return seq_copy(dq_out.at[j], dq_in, dq_send, dq_recv, j, behind(j))

    def inner_q_copy(j):
        return head_copy(inner_q, iq_send, iq_recv, j)

    def inner_k_copy(j):
        return head_copy(inner_k, ik_send, ik_recv, j)

    each(1, n_h, lambda j: squares_copy(j).start())
    each(1, n_s, lambda j: deltas_copy(j).start())
    each(1, n_s, lambda j: grads_copy(j).start())

    each(1, n_h, lambda j: squares_copy(j).wait_recv())
    rates = lax.rsqrt(jnp.sum(squares[...], axis=0) / features + EPSILON)
    q_rate, k_rate = rates[0:1], rates[1:2]
    queries[0] = (x_t[...] * q_rate * qg_t[...]).astype(jnp.bfloat16)
    each(1, n_s, lambda j: queries_copy(j).start())
    k_norm = y_t[...] * k_rate * kg_t[...]
    keys_t[...] = k_norm.astype(jnp.bfloat16)
    keys[...] = k_norm.T.astype(jnp.bfloat16)
    own_group = order[me]

    def group(j):
        if not (isinstance(j, int) and j == 0):
            grads_copy(j).wait_recv()
            deltas_copy(j).wait_recv()
        dprobs = dot(values[...], grads[j], NN) - deltas[j]
        if not (isinstance(j, int) and j == 0):
            queries_copy(j).wait_recv()
        source = behind(j)
        bias = jnp.where(order[source] >= own_group, 0.0, HIDDEN).astype(jnp.float32)
        scores = dot(keys[...], queries[j], NN) * root
        top = jnp.max(scores, axis=0, keepdims=True)
        probs = jnp.exp(scores - top)
        total = jnp.sum(probs, axis=0, keepdims=True)
        ds = probs * dprobs
        ds_low = ds.astype(jnp.bfloat16)
        exps[j] = probs.astype(jnp.bfloat16)
        dscore[j] = ds_low
        share = 1.0 / total
        moment = jnp.sum(ds * scores, axis=0, keepdims=True) * share
        maxes[j] = top + bias
        stats[0, source, 0:1] = top + bias + jnp.log(total)
        stats[0, source, 1:2] = moment
        dq_out[j] = (dot(keys_t[...], ds_low, NN) * (share * root)).astype(jnp.bfloat16)
        if not (isinstance(j, int) and j == 0):
            dq_copy(j).start()

    group(0)
    each(1, n_s, group)

    each(1, n_s, lambda j: stats_copy(j).start())
    each(1, n_s, lambda j: stats_copy(j).wait_recv())

    def log_total(g):
        logs = [stats[j, g, 0:1] for j in range(n_s)]
        peak = functools.reduce(jnp.maximum, logs)
        return peak + jnp.log(sum(jnp.exp(value - peak) for value in logs))

    own_log = log_total(me)
    weights = [jnp.exp(stats[j, me, 0:1] - own_log) for j in range(n_s)]
    inner_q[0] = sum(weights[j] * stats[j, me, 1:2] for j in range(n_s))
    each(1, n_h, lambda j: inner_q_copy(j).start())

    def key_side(j):
        scale = jnp.exp(maxes[j] - log_total(behind(j)))
        query = (queries[j].astype(jnp.float32) * scale).astype(jnp.bfloat16)
        grad_out = (grads[j].astype(jnp.float32) * scale).astype(jnp.bfloat16)
        dk_add = dot(dscore[j], query, NT)
        dv_add = dot(exps[j], grad_out, NT)
        if isinstance(j, int) and j == 0:
            dk_sum[...] = dk_add
            dv_sum[...] = dv_add
        else:
            dk_sum[...] += dk_add
            dv_sum[...] += dv_add

    key_side(0)
    each(1, n_s, key_side)
    gk = (dk_sum[...] * root).T * kg_t[...]
    inner_k[0] = jnp.sum(gk * y_t[...], axis=0, keepdims=True)
    each(1, n_h, lambda j: inner_k_copy(j).start())
    d_v[...] = dv_sum[...].astype(jnp.bfloat16)

    each(1, n_h, lambda j: inner_q_copy(j).wait_recv())
    each(1, n_h, lambda j: inner_k_copy(j).wait_recv())
    k_total = jnp.sum(inner_k[...], axis=0)
    grad_k = k_rate * gk - y_t[...] * (k_rate * k_rate * k_rate * k_total / features)
    d_k[...] = grad_k.T.astype(jnp.bfloat16)

    q_total = jnp.sum(inner_q[...], axis=0)
    dq = dq_out[0].astype(jnp.float32) * weights[0]
    for j in range(1, n_s):
        dq_copy(j).wait_recv()
        dq = dq + dq_in[j].astype(jnp.float32) * weights[inverse(j)]
    grad_q = q_rate * (dq * qg_t[...]) - x_t[...] * (q_rate * q_rate * q_total / features)
    d_q[...] = grad_q.T.astype(jnp.bfloat16)

    each(1, n_h, lambda j: squares_copy(j).wait_send())
    each(1, n_s, lambda j: grads_copy(j).wait_send())
    each(1, n_s, lambda j: deltas_copy(j).wait_send())
    each(1, n_s, lambda j: queries_copy(j).wait_send())
    each(1, n_s, lambda j: stats_copy(j).wait_send())
    each(1, n_s, lambda j: dq_copy(j).wait_send())
    each(1, n_h, lambda j: inner_q_copy(j).wait_send())
    each(1, n_h, lambda j: inner_k_copy(j).wait_send())


def local(n_s, n_h, q_raw, k_raw, values, out, d_out, q_gain, k_gain, order):
    rows, width = q_raw.shape
    block = jax.ShapeDtypeStruct((rows, width), jnp.bfloat16)
    vmem = pl.BlockSpec(memory_space=pltpu.VMEM)
    smem = pl.BlockSpec(memory_space=pltpu.SMEM)
    low, wide = jnp.bfloat16, jnp.float32
    sems = []
    for count in (n_h, n_s, n_s, n_s, n_s, n_s, n_h, n_h):
        sems += [pltpu.SemaphoreType.DMA((count,))] * 2
    return pl.pallas_call(
        functools.partial(kernel, n_s, n_h),
        out_shape=(block, block, block),
        in_specs=[smem] + [vmem] * 7,
        out_specs=(vmem, vmem, vmem),
        scratch_shapes=[
            pltpu.VMEM((width, rows), wide),
            pltpu.VMEM((width, rows), wide),
            pltpu.VMEM((width, rows), wide),
            pltpu.VMEM((width, rows), wide),
            pltpu.VMEM((rows, width), low),
            pltpu.VMEM((width, rows), low),
            pltpu.VMEM((n_s, rows, rows), low),
            pltpu.VMEM((n_s, rows, rows), low),
            pltpu.VMEM((n_s, 1, rows), wide),
            pltpu.VMEM((rows, width), wide),
            pltpu.VMEM((rows, width), wide),
            pltpu.VMEM((n_h, 2, rows), wide),
            pltpu.VMEM((n_s, width, rows), low),
            pltpu.VMEM((n_s, 1, rows), wide),
            pltpu.VMEM((n_s, width, rows), low),
            pltpu.VMEM((n_s, n_s, 2, rows), wide),
            pltpu.VMEM((n_s, width, rows), low),
            pltpu.VMEM((n_s, width, rows), low),
            pltpu.VMEM((n_h, 1, rows), wide),
            pltpu.VMEM((n_h, 1, rows), wide),
        ]
        + sems,
        compiler_params=pltpu.CompilerParams(
            collective_id=0, has_side_effects=True, vmem_limit_bytes=40 * 1024 * 1024
        ),
        cost_estimate=pl.CostEstimate(
            flops=10 * n_s * rows * rows * width,
            bytes_accessed=16 * rows * width,
            transcendentals=n_s * rows * rows,
        ),
    )(
        order,
        q_raw,
        k_raw,
        values,
        out,
        d_out,
        q_gain.reshape(1, width),
        k_gain.reshape(1, width),
    )


def solution(mesh):
    block = P("seq", "head")
    return jax.shard_map(
        functools.partial(local, mesh.shape["seq"], mesh.shape["head"]),
        mesh=mesh,
        in_specs=(block, block, block, block, block, P("head"), P("head"), P()),
        out_specs=(block, block, block),
        check_vma=False,
    )
```

time: 107 us -> 36.1 us (0.34)
  blocking collectives: 31.7 us -> 0 us
  Pallas kernels: 0 us -> 28.1 us
  waiting for transfers between devices: 24.7 us -> 0 us
  starting transfers between devices: 20.7 us -> 0 us
  loops' own time: 7.6 us -> 0 us
  matrix products: 6.5 us -> 0 us
  other arithmetic: 5.65 us -> 0 us
  between operations: 2.13 us -> 0.67 us
    psum x2 -> x0, blocking collectives: 31.7 us -> none  [the longest x1 18.1 us: local(): lax.psum((jnp.sum(q_float * q_float, axis=1), jnp.sum(k_float * k_float,...]
    pallas_call x0 -> x1, Pallas kernels: none -> 28.1 us  [local(): pl.pallas_call(functools.partial(kernel, n_s, n_h), out_shape=(block, blo...]
    ppermute x17 -> x0, waiting for transfers between devices: 24.7 us -> none  [from_behind(): return lax.ppermute(value, axis, pairs)]
    ppermute x17 -> x0, starting transfers between devices: 20.7 us -> none  [from_behind(): return lax.ppermute(value, axis, pairs)]
    another operation x2 -> x0, loops' own time: 7.6 us -> none  [the longest x1 3.92 us: local(): lax.fori_loop(0, cycle_size - 1, key_turn, (k_norm, values, zeros_block,...]
    dot_general x24 -> x0, matrix products: 6.5 us -> none  [the longest x8 2.17 us: compute(): jnp.dot(queries, keys.T, preferred_element_type=jnp.float32)]
    reduce_sum x11 -> x0, other arithmetic: 4.91 us -> none  [the longest x7 4.57 us: lookup(): jnp.sum(jnp.where(jnp.arange(table.shape[0], dtype=jnp.int32) == index, t...]
    unnamed x24 -> x19, local copies, waits for them, and re-layouts: 7 us -> 7.05 us
  transfers between devices with their start and end apart: 17 -> 0, of which waited for: 10 -> 0; matrix products, arithmetic and copies ran while one was open for 11% -> 0% of each run, Pallas kernels for 0% -> 0%
where the time goes in v1:
time: 36.1 us; the launch traced here: 35.9 us
  Pallas kernels  28.1 us (78%)
  local copies, waits for them, and re-layouts  7.05 us (20%)
  between operations  0.67 us (2%)
    pallas_call x1, Pallas kernels, local(): pl.pallas_call(functools.partial(kernel, n_s, n_h), out_shape=(block, blo...  28.1 us
    unnamed x19, local copies, waits for them, and re-layouts  7.05 us

profile of v1, /device:TPU:0, one launch (start us, length us, event | category | flops | bytes accessed | tf_op | source)
XLA Modules:
  0.0 35.9 jit_solution(5603992445033724273)
XLA Ops:
  0.6 0.0 copy-start.5
  0.6 0.0 copy-start.6
  0.7 0.0 copy-start.7
  0.7 0.6 %copy-done.5 = s32[4]{0:T(128)S(1)} copy-done((s32[4]{0:T(128)S(1)}, s32[4]{0:T(128)}, u32[]{:S(2)}) %copy-start.5) | copy-done | bytes 40
  1.3 0.0 copy-done.6
  1.3 0.0 copy-done.7
  1.3 0.0 copy-start
  1.3 0.9 %copy-done = bf16[384,128]{1,0:T(8,128)(2,1)S(1)} copy-done((bf16[384,128]{1,0:T(8,128)(2,1)S(1)}, bf16[384,128]{1,0:T(8,128)(2,1)}, u32[]{:S(2)}) %copy-start) | copy-done | bytes 98328
  2.2 0.0 copy-start.1
  2.2 0.9 %copy-done.1 = bf16[384,128]{1,0:T(8,128)(2,1)S(1)} copy-done((bf16[384,128]{1,0:T(8,128)(2,1)S(1)}, bf16[384,128]{1,0:T(8,128)(2,1)}, u32[]{:S(2)}) %copy-start.1) | copy-done | bytes 98328
  3.1 0.0 copy-start.2
  3.1 0.9 %copy-done.2 = bf16[384,128]{1,0:T(8,128)(2,1)S(1)} copy-done((bf16[384,128]{1,0:T(8,128)(2,1)S(1)}, bf16[384,128]{1,0:T(8,128)(2,1)}, u32[]{:S(2)}) %copy-start.2) | copy-done | bytes 98328
  4.0 0.0 copy-start.3
  4.0 0.9 %copy-done.3 = bf16[384,128]{1,0:T(8,128)(2,1)S(1)} copy-done((bf16[384,128]{1,0:T(8,128)(2,1)S(1)}, bf16[384,128]{1,0:T(8,128)(2,1)}, u32[]{:S(2)}) %copy-start.3) | copy-done | bytes 98328
  4.9 0.0 copy-start.4
  4.9 0.9 %copy-done.4 = bf16[384,128]{1,0:T(8,128)(2,1)S(1)} copy-done((bf16[384,128]{1,0:T(8,128)(2,1)S(1)}, bf16[384,128]{1,0:T(8,128)(2,1)}, u32[]{:S(2)}) %copy-start.4) | copy-done | bytes 98328
  5.8 28.1 %shard_map.103 = (bf16[384,128]{1,0:T(8,128)(2,1)S(1)}, bf16[384,128]{1,0:T(8,128)(2,1)S(1)}, bf16[384,128]{1,0:T(8,128)(2,1)S(1)}) custom-call(s32[4]{0:T(128)S(1)} %copy-done.5, bf16[384,128]{1,0:T(8,128)(2,1)S(1)} %copy-done, bf16[384,128]{1,0:T(8,128)(2,1)S(1)} %copy-done.1, bf16[384,128]{1,0:T(8,128)(2,1)S(1)} %copy-done.2, ...), custom_call_target="tpu_custom_call" | custom-call | flops 754974720 | bytes 786432 | tf_op jit(solution)/shard_map/pallas_call | solution.py:295
  33.9 0.6 %copy.14 = bf16[384,128]{1,0:T(8,128)(2,1)} copy(bf16[384,128]{1,0:T(8,128)(2,1)S(1)} %get-tuple-element.6) | data formatting | bytes 196608
  34.6 0.6 %copy.15 = bf16[384,128]{1,0:T(8,128)(2,1)} copy(bf16[384,128]{1,0:T(8,128)(2,1)S(1)} %get-tuple-element.7) | data formatting | bytes 196608
  35.2 0.6 %copy.16 = bf16[384,128]{1,0:T(8,128)(2,1)} copy(bf16[384,128]{1,0:T(8,128)(2,1)S(1)} %get-tuple-element.8) | data formatting | bytes 196608
Async XLA Ops:
  0.6 0.7 %copy-start.5 = (s32[4]{0:T(128)S(1)}, s32[4]{0:T(128)}, u32[]{:S(2)}) copy-start(s32[4]{0:T(128)} %order.1) | copy-start | bytes 52
  0.6 0.7 %copy-start.6 = (bf16[128]{0:T(256)(128)(2,1)S(1)}, bf16[128]{0:T(256)(128)(2,1)}, u32[]{:S(2)}) copy-start(bf16[128]{0:T(256)(128)(2,1)} %param.13) | copy-start | bytes 772
  0.7 0.7 %copy-start.7 = (bf16[128]{0:T(256)(128)(2,1)S(1)}, bf16[128]{0:T(256)(128)(2,1)}, u32[]{:S(2)}) copy-start(bf16[128]{0:T(256)(128)(2,1)} %param.14) | copy-start | bytes 772
  1.3 0.9 %copy-start = (bf16[384,128]{1,0:T(8,128)(2,1)S(1)}, bf16[384,128]{1,0:T(8,128)(2,1)}, u32[]{:S(2)}) copy-start(bf16[384,128]{1,0:T(8,128)(2,1)} %q_raw.1) | copy-start | bytes 294916
  2.2 0.9 %copy-start.1 = (bf16[384,128]{1,0:T(8,128)(2,1)S(1)}, bf16[384,128]{1,0:T(8,128)(2,1)}, u32[]{:S(2)}) copy-start(bf16[384,128]{1,0:T(8,128)(2,1)} %k_raw.1) | copy-start | bytes 294916
  3.1 0.9 %copy-start.2 = (bf16[384,128]{1,0:T(8,128)(2,1)S(1)}, bf16[384,128]{1,0:T(8,128)(2,1)}, u32[]{:S(2)}) copy-start(bf16[384,128]{1,0:T(8,128)(2,1)} %values.1) | copy-start | bytes 294916
  4.0 0.9 %copy-start.3 = (bf16[384,128]{1,0:T(8,128)(2,1)S(1)}, bf16[384,128]{1,0:T(8,128)(2,1)}, u32[]{:S(2)}) copy-start(bf16[384,128]{1,0:T(8,128)(2,1)} %out.1) | copy-start | bytes 294916
  4.9 0.9 %copy-start.4 = (bf16[384,128]{1,0:T(8,128)(2,1)S(1)}, bf16[384,128]{1,0:T(8,128)(2,1)}, u32[]{:S(2)}) copy-start(bf16[384,128]{1,0:T(8,128)(2,1)} %d_out.1) | copy-start | bytes 294916

commit v2 on v1

v2 whole, which is shorter than its diff:
```python
import functools
import math

import jax
import jax.numpy as jnp
from jax import lax
from jax.experimental import pallas as pl
from jax.experimental.pallas import tpu as pltpu
from jax.sharding import PartitionSpec as P

EPSILON = 1e-06
HIDDEN = -1e30
LOG2E = math.log2(math.e)
MESH = pl.DeviceIdType.MESH
NN = (((1,), (0,)), ((), ()))
NT = (((1,), (1,)), ((), ()))


def dot(a, b, dims):
    return lax.dot_general(a, b, dims, preferred_element_type=jnp.float32)


def each(low, high, body):
    if high - low <= 8:
        for j in range(low, high):
            body(j)
    else:

        def step(j, carry):
            body(j)
            return carry

        lax.fori_loop(low, high, step, 0)


def kernel(
    n_s,
    n_h,
    order_hbm,
    q_hbm,
    k_hbm,
    v_hbm,
    o_hbm,
    do_hbm,
    qg_hbm,
    kg_hbm,
    d_q,
    d_k,
    d_v,
    order,
    q_raw,
    k_raw,
    values,
    out,
    d_out,
    q_gain,
    k_gain,
    x_t,
    y_t,
    qg_t,
    kg_t,
    keys,
    keys_t,
    scores,
    dk_sum,
    dv_sum,
    squares,
    raws,
    queries,
    rows_in,
    grads,
    totals,
    moments,
    dq_out,
    dq_in,
    inner_q,
    inner_k,
    load,
    sq_send,
    sq_recv,
    ra_send,
    ra_recv,
    ro_send,
    ro_recv,
    gr_send,
    gr_recv,
    to_send,
    to_recv,
    mo_send,
    mo_recv,
    dq_send,
    dq_recv,
    iq_send,
    iq_recv,
    ik_send,
    ik_recv,
):
    rows, width = q_raw.shape
    features = n_h * width
    root = width ** (-0.5)
    side = math.isqrt(n_s) if math.isqrt(n_s) ** 2 == n_s else n_s
    tall = n_s // side
    me = lax.axis_index("seq")
    mine = lax.axis_index("head")
    my_y, my_x = lax.div(me, side), lax.rem(me, side)

    def parts(j):
        if isinstance(j, int):
            return j // side, j % side
        return lax.div(j, side), lax.rem(j, side)

    def ahead(j):
        jy, jx = parts(j)
        return lax.rem(my_y + jy, tall) * side + lax.rem(my_x + jx, side)

    def behind(j):
        jy, jx = parts(j)
        return lax.rem(my_y + tall - jy, tall) * side + lax.rem(my_x + side - jx, side)

    def inverse(j):
        jy, jx = parts(j)
        if isinstance(j, int):
            return ((tall - jy) % tall) * side + (side - jx) % side
        return lax.rem(tall - jy, tall) * side + lax.rem(side - jx, side)

    def head_ahead(j):
        return lax.rem(mine + j, n_h)

    def seq_copy(src, dst, send, recv, j, peer):
        return pltpu.make_async_remote_copy(
            src_ref=src,
            dst_ref=dst.at[j],
            send_sem=send.at[j],
            recv_sem=recv.at[j],
            device_id=(peer, mine),
            device_id_type=MESH,
        )

    def head_copy(buffer, send, recv, j):
        return pltpu.make_async_remote_copy(
            src_ref=buffer.at[0],
            dst_ref=buffer.at[j],
            send_sem=send.at[j],
            recv_sem=recv.at[j],
            device_id=(me, head_ahead(j)),
            device_id_type=MESH,
        )

    barrier = pltpu.get_barrier_semaphore()

    def greet_seq(j):
        pl.semaphore_signal(barrier, inc=1, device_id=(ahead(j), mine), device_id_type=MESH)

    def greet_head(j):
        pl.semaphore_signal(barrier, inc=1, device_id=(me, head_ahead(j)), device_id_type=MESH)

    each(1, n_s, greet_seq)
    each(1, n_h, greet_head)

    loads = [
        pltpu.make_async_copy(src, dst, load.at[i])
        for i, (src, dst) in enumerate(
            (
                (q_hbm, q_raw),
                (k_hbm, k_raw),
                (do_hbm, d_out),
                (o_hbm, out),
                (qg_hbm, q_gain),
                (kg_hbm, k_gain),
                (v_hbm, values),
                (order_hbm, order),
            )
        )
    ]
    for copy in loads:
        copy.start()

    loads[0].wait()
    x = q_raw[...].astype(jnp.float32).T
    x_t[...] = x
    raws[0] = x.astype(jnp.bfloat16)
    squares[0, 0:1] = jnp.sum(x * x, axis=0, keepdims=True)
    loads[1].wait()
    y = k_raw[...].astype(jnp.float32).T
    y_t[...] = y
    squares[0, 1:2] = jnp.sum(y * y, axis=0, keepdims=True)

    pl.semaphore_wait(barrier, n_s - 1 + n_h - 1)

    def squares_copy(j):
        return head_copy(squares, sq_send, sq_recv, j)

    def raws_copy(j):
        return seq_copy(raws.at[0], raws, ra_send, ra_recv, j, ahead(j))

    def rows_copy(j):
        return seq_copy(rows_in.at[0], rows_in, ro_send, ro_recv, j, ahead(j))

    def grads_copy(j):
        return seq_copy(grads.at[0], grads, gr_send, gr_recv, j, ahead(j))

    def totals_copy(j):
        return seq_copy(totals.at[0], totals, to_send, to_recv, j, ahead(j))

    def moments_copy(j):
        return seq_copy(moments.at[0, j], moments.at[1], mo_send, mo_recv, j, behind(j))

    def dq_copy(j):
        return seq_copy(dq_out.at[j], dq_in, dq_send, dq_recv, j, behind(j))

    def inner_q_copy(j):
        return head_copy(inner_q, iq_send, iq_recv, j)

    def inner_k_copy(j):
        return head_copy(inner_k, ik_send, ik_recv, j)

    each(1, n_h, lambda j: squares_copy(j).start())
    each(1, n_s, lambda j: raws_copy(j).start())

    loads[2].wait()
    loads[3].wait()
    grad = d_out[...].astype(jnp.float32)
    grads[0] = grad.T.astype(jnp.bfloat16)
    rows_in[0, 1:2] = jnp.sum((grad * out[...].astype(jnp.float32)).T, axis=0, keepdims=True)
    loads[4].wait()
    loads[5].wait()
    qg_t[...] = jnp.broadcast_to(q_gain[...].astype(jnp.float32), (rows, width)).T
    kg_t[...] = jnp.broadcast_to(k_gain[...].astype(jnp.float32), (rows, width)).T

    each(1, n_h, lambda j: squares_copy(j).wait_recv())
    rates = lax.rsqrt(jnp.sum(squares[...], axis=0) / features + EPSILON)
    q_rate, k_rate = rates[0:1], rates[1:2]
    rows_in[0, 0:1] = q_rate
    each(1, n_s, lambda j: rows_copy(j).start())
    each(1, n_s, lambda j: grads_copy(j).start())

    k_norm = y_t[...] * k_rate * kg_t[...]
    keys_t[...] = k_norm.astype(jnp.bfloat16)
    keys[...] = k_norm.T.astype(jnp.bfloat16)
    loads[6].wait()
    loads[7].wait()
    own_group = order[me]

    def hidden(source):
        return jnp.where(order[source] >= own_group, 0.0, HIDDEN).astype(jnp.float32)

    def own(j):
        return isinstance(j, int) and j == 0

    def total_turn(j):
        if not own(j):
            raws_copy(j).wait_recv()
            rows_copy(j).wait_recv()
        query = raws[j].astype(jnp.float32) * rows_in[j, 0:1] * qg_t[...]
        queries[j] = query.astype(jnp.bfloat16)
        source = behind(j)
        score = dot(keys[...], queries[j], NN) * (root * LOG2E) + hidden(source)
        scores[j] = score
        totals[0, source] = jnp.sum(jnp.exp2(score), axis=0, keepdims=True)

    total_turn(0)
    each(1, n_s, total_turn)
    each(1, n_s, lambda j: totals_copy(j).start())
    each(1, n_s, lambda j: totals_copy(j).wait_recv())

    def grad_turn(j):
        if not own(j):
            grads_copy(j).wait_recv()
        source = behind(j)
        log_total = jnp.log2(sum(totals[i, source] for i in range(n_s)))
        score = scores[j]
        probs = jnp.exp2(score - log_total)
        ds = probs * (dot(values[...], grads[j], NN) - rows_in[j, 1:2])
        ds_low = ds.astype(jnp.bfloat16)
        moments[0, j] = jnp.sum(ds * score, axis=0, keepdims=True) * (1.0 / LOG2E)
        if not own(j):
            moments_copy(j).start()
        dq_out[j] = (dot(keys_t[...], ds_low, NN) * root).astype(jnp.bfloat16)
        if not own(j):
            dq_copy(j).start()
        dk_add = dot(ds_low, queries[j], NT)
        dv_add = dot(probs.astype(jnp.bfloat16), grads[j], NT)
        if own(j):
            dk_sum[...] = dk_add
            dv_sum[...] = dv_add
        else:
            dk_sum[...] += dk_add
            dv_sum[...] += dv_add

    grad_turn(0)
    each(1, n_s, grad_turn)

    gk = (dk_sum[...] * root).T * kg_t[...]
    inner_k[0] = jnp.sum(gk * y_t[...], axis=0, keepdims=True)
    each(1, n_h, lambda j: inner_k_copy(j).start())
    each(1, n_s, lambda j: moments_copy(j).wait_recv())
    inner_q[0] = moments[0, 0] + sum(moments[1, j] for j in range(1, n_s))
    each(1, n_h, lambda j: inner_q_copy(j).start())
    d_v[...] = dv_sum[...].astype(jnp.bfloat16)

    each(1, n_h, lambda j: inner_k_copy(j).wait_recv())
    k_total = jnp.sum(inner_k[...], axis=0)
    grad_k = k_rate * gk - y_t[...] * (k_rate * k_rate * k_rate * k_total / features)
    d_k[...] = grad_k.T.astype(jnp.bfloat16)

    dq = dq_out[0].astype(jnp.float32)
    for j in range(1, n_s):
        dq_copy(j).wait_recv()
        dq = dq + dq_in[j].astype(jnp.float32)
    each(1, n_h, lambda j: inner_q_copy(j).wait_recv())
    q_total = jnp.sum(inner_q[...], axis=0)
    grad_q = q_rate * (dq * qg_t[...]) - x_t[...] * (q_rate * q_rate * q_total / features)
    d_q[...] = grad_q.T.astype(jnp.bfloat16)

    each(1, n_h, lambda j: squares_copy(j).wait_send())
    each(1, n_s, lambda j: raws_copy(j).wait_send())
    each(1, n_s, lambda j: rows_copy(j).wait_send())
    each(1, n_s, lambda j: grads_copy(j).wait_send())
    each(1, n_s, lambda j: totals_copy(j).wait_send())
    each(1, n_s, lambda j: moments_copy(j).wait_send())
    each(1, n_s, lambda j: dq_copy(j).wait_send())
    each(1, n_h, lambda j: inner_q_copy(j).wait_send())
    each(1, n_h, lambda j: inner_k_copy(j).wait_send())


def deliver(*refs):
    sems = refs[6]
    copies = [pltpu.make_async_copy(refs[i], refs[i + 3], sems.at[i]) for i in range(3)]
    for copy in copies:
        copy.start()
    for copy in copies:
        copy.wait()


def local(n_s, n_h, q_raw, k_raw, values, out, d_out, q_gain, k_gain, order):
    rows, width = q_raw.shape
    block = jax.ShapeDtypeStruct((rows, width), jnp.bfloat16)
    vmem = pl.BlockSpec(memory_space=pltpu.VMEM)
    hbm = pl.BlockSpec(memory_space=pltpu.HBM)
    low, wide = jnp.bfloat16, jnp.float32
    sems = [pltpu.SemaphoreType.DMA((8,))]
    for count in (n_h, n_s, n_s, n_s, n_s, n_s, n_s, n_h, n_h):
        sems += [pltpu.SemaphoreType.DMA((count,))] * 2
    results = pl.pallas_call(
        functools.partial(kernel, n_s, n_h),
        out_shape=(block, block, block),
        in_specs=[hbm] * 8,
        out_specs=(vmem, vmem, vmem),
        scratch_shapes=[
            pltpu.SMEM((n_s,), jnp.int32),
            pltpu.VMEM((rows, width), low),
            pltpu.VMEM((rows, width), low),
            pltpu.VMEM((rows, width), low),
            pltpu.VMEM((rows, width), low),
            pltpu.VMEM((rows, width), low),
            pltpu.VMEM((1, width), low),
            pltpu.VMEM((1, width), low),
            pltpu.VMEM((width, rows), wide),
            pltpu.VMEM((width, rows), wide),
            pltpu.VMEM((width, rows), wide),
            pltpu.VMEM((width, rows), wide),
            pltpu.VMEM((rows, width), low),
            pltpu.VMEM((width, rows), low),
            pltpu.VMEM((n_s, rows, rows), wide),
            pltpu.VMEM((rows, width), wide),
            pltpu.VMEM((rows, width), wide),
            pltpu.VMEM((n_h, 2, rows), wide),
            pltpu.VMEM((n_s, width, rows), low),
            pltpu.VMEM((n_s, width, rows), low),
            pltpu.VMEM((n_s, 2, rows), wide),
            pltpu.VMEM((n_s, width, rows), low),
            pltpu.VMEM((n_s, n_s, 1, rows), wide),
            pltpu.VMEM((2, n_s, 1, rows), wide),
            pltpu.VMEM((n_s, width, rows), low),
            pltpu.VMEM((n_s, width, rows), low),
            pltpu.VMEM((n_h, 1, rows), wide),
            pltpu.VMEM((n_h, 1, rows), wide),
        ]
        + sems,
        compiler_params=pltpu.CompilerParams(
            collective_id=0, has_side_effects=True, vmem_limit_bytes=40 * 1024 * 1024
        ),
        cost_estimate=pl.CostEstimate(
            flops=10 * n_s * rows * rows * width,
            bytes_accessed=16 * rows * width,
            transcendentals=2 * n_s * rows * rows,
        ),
    )(
        *(
            pltpu.with_memory_space_constraint(array, pltpu.HBM)
            for array in (
                order,
                q_raw,
                k_raw,
                values,
                out,
                d_out,
                q_gain.reshape(1, width),
                k_gain.reshape(1, width),
            )
        )
    )
    return pl.pallas_call(
        deliver,
        out_shape=(block, block, block),
        in_specs=[vmem] * 3,
        out_specs=(hbm, hbm, hbm),
        scratch_shapes=[pltpu.SemaphoreType.DMA((3,))],
    )(*results)


def solution(mesh):
    block = P("seq", "head")
    return jax.shard_map(
        functools.partial(local, mesh.shape["seq"], mesh.shape["head"]),
        mesh=mesh,
        in_specs=(block, block, block, block, block, P("head"), P("head"), P()),
        out_specs=(block, block, block),
        check_vma=False,
    )
```

time: 36.1 us -> 31.2 us (0.86)
  local copies, waits for them, and re-layouts: 7.05 us -> 1.89 us
  Pallas kernels: 28.1 us -> 28.5 us
    unnamed x19 -> x6, local copies, waits for them, and re-layouts: 7.05 us -> 1.89 us
    pallas_call x0 -> x1, Pallas kernels: none -> 1.72 us  [local(): pl.pallas_call(deliver, out_shape=(block, block, block), in_specs=[vmem]...]
    pallas_call x1, Pallas kernels: 28.1 us -> 26.8 us  [local(): pl.pallas_call(functools.partial(kernel, n_s, n_h), out_shape=(block, blo...]
where the time goes in v2:
time: 31.2 us; the launch traced here: 31 us
  Pallas kernels  28.5 us (91%)
  local copies, waits for them, and re-layouts  1.89 us (6%)
  between operations  0.65 us (2%)
    pallas_call x1, Pallas kernels, local(): pl.pallas_call(functools.partial(kernel, n_s, n_h), out_shape=(block, blo...  26.8 us
    unnamed x6, local copies, waits for them, and re-layouts  1.89 us
    pallas_call x1, Pallas kernels, local(): pl.pallas_call(deliver, out_shape=(block, block, block), in_specs=[vmem]...  1.72 us

profile of v2, /device:TPU:0, one launch (start us, length us, event | category | flops | bytes accessed | tf_op | source)
XLA Modules:
  0.0 31.0 jit_solution(15294492042603901116)
XLA Ops:
  0.6 26.8 %shard_map.103 = (bf16[384,128]{1,0:T(8,128)(2,1)S(1)}, bf16[384,128]{1,0:T(8,128)(2,1)S(1)}, bf16[384,128]{1,0:T(8,128)(2,1)S(1)}) custom-call(s32[4]{0:T(128)} %order_hbm.1, bf16[384,128]{1,0:T(8,128)(2,1)} %q_hbm.1, bf16[384,128]{1,0:T(8,128)(2,1)} %k_hbm.1, bf16[384,128]{1,0:T(8,128)(2,1)} %v_hbm.1, bf16[384,128]{1,0:T(8,128)(2,1)} %o_hbm.1, ...), custom_call_target="tpu_custom_call" | custom-call | flops 754974720 | bytes 786432 | tf_op jit(solution)/shard_map/pallas_call | solution.py:344
  27.4 0.0 copy-start
  27.4 0.6 %copy-done = bf16[384,128]{1,0:T(8,128)(2,1)} copy-done((bf16[384,128]{1,0:T(8,128)(2,1)}, bf16[384,128]{1,0:T(8,128)(2,1)S(1)}, u32[]{:S(2)}) %copy-start) | copy-done | bytes 98328
  28.0 0.0 copy-start.1
  28.0 0.6 %copy-done.1 = bf16[384,128]{1,0:T(8,128)(2,1)} copy-done((bf16[384,128]{1,0:T(8,128)(2,1)}, bf16[384,128]{1,0:T(8,128)(2,1)S(1)}, u32[]{:S(2)}) %copy-start.1) | copy-done | bytes 98328
  28.7 0.0 copy-start.2
  28.7 0.6 %copy-done.2 = bf16[384,128]{1,0:T(8,128)(2,1)} copy-done((bf16[384,128]{1,0:T(8,128)(2,1)}, bf16[384,128]{1,0:T(8,128)(2,1)S(1)}, u32[]{:S(2)}) %copy-start.2) | copy-done | bytes 98328
  29.3 1.7 %shard_map.104 = (bf16[384,128]{1,0:T(8,128)(2,1)}, bf16[384,128]{1,0:T(8,128)(2,1)}, bf16[384,128]{1,0:T(8,128)(2,1)}) custom-call(bf16[384,128]{1,0:T(8,128)(2,1)} %copy-done, bf16[384,128]{1,0:T(8,128)(2,1)} %copy-done.1, bf16[384,128]{1,0:T(8,128)(2,1)} %copy-done.2), custom_call_target="tpu_custom_call" | custom-call | tf_op jit(solution)/shard_map/pallas_call | solution.py:403
Async XLA Ops:
  27.4 0.6 %copy-start = (bf16[384,128]{1,0:T(8,128)(2,1)}, bf16[384,128]{1,0:T(8,128)(2,1)S(1)}, u32[]{:S(2)}) copy-start(bf16[384,128]{1,0:T(8,128)(2,1)S(1)} %get-tuple-element.6.refs_0_) | copy-start | bytes 294916
  28.0 0.6 %copy-start.1 = (bf16[384,128]{1,0:T(8,128)(2,1)}, bf16[384,128]{1,0:T(8,128)(2,1)S(1)}, u32[]{:S(2)}) copy-start(bf16[384,128]{1,0:T(8,128)(2,1)S(1)} %get-tuple-element.7.refs_1_) | copy-start | bytes 294916
  28.7 0.6 %copy-start.2 = (bf16[384,128]{1,0:T(8,128)(2,1)}, bf16[384,128]{1,0:T(8,128)(2,1)S(1)}, u32[]{:S(2)}) copy-start(bf16[384,128]{1,0:T(8,128)(2,1)S(1)} %get-tuple-element.8.refs_2_) | copy-start | bytes 294916

commit v3 on v2

v3 whole, which is shorter than its diff:
```python
import functools
import math

import jax
import jax.numpy as jnp
from jax import lax
from jax.experimental import pallas as pl
from jax.experimental.pallas import tpu as pltpu
from jax.sharding import PartitionSpec as P

EPSILON = 1e-06
HIDDEN = -1e30
LOG2E = math.log2(math.e)
MESH = pl.DeviceIdType.MESH
NN = (((1,), (0,)), ((), ()))
NT = (((1,), (1,)), ((), ()))


def dot(a, b, dims):
    return lax.dot_general(a, b, dims, preferred_element_type=jnp.float32)


def each(low, high, body):
    if high - low <= 8:
        for j in range(low, high):
            body(j)
    else:

        def step(j, carry):
            body(j)
            return carry

        lax.fori_loop(low, high, step, 0)


def grid_of(n_s):
    root = math.isqrt(n_s)
    return (root, root) if root * root == n_s else (n_s, 1)


def kernel(
    n_s,
    n_h,
    order_hbm,
    q_hbm,
    k_hbm,
    v_hbm,
    o_hbm,
    do_hbm,
    qg_hbm,
    kg_hbm,
    d_q,
    d_k,
    d_v,
    order,
    q_raw,
    k_raw,
    out,
    d_out,
    q_gain,
    k_gain,
    x_t,
    q_scale,
    k_scale,
    qg_t,
    kg_t,
    keys,
    keys_t,
    queries,
    scores,
    squares,
    q_in,
    k_in,
    q_rows,
    k_rows,
    grads,
    values,
    totals,
    q_moment,
    k_moment,
    dq_out,
    dq_in,
    dk_out,
    dk_in,
    dv_out,
    dv_in,
    inner,
    load,
    sq_send,
    sq_recv,
    qi_send,
    qi_recv,
    ki_send,
    ki_recv,
    qr_send,
    qr_recv,
    kr_send,
    kr_recv,
    gr_send,
    gr_recv,
    va_send,
    va_recv,
    to_send,
    to_recv,
    qm_send,
    qm_recv,
    km_send,
    km_recv,
    dq_send,
    dq_recv,
    dk_send,
    dk_recv,
    dv_send,
    dv_recv,
    inn_send,
    inn_recv,
):
    rows, width = q_raw.shape
    features = n_h * width
    root = width ** (-0.5)
    side, tall = grid_of(n_s)
    me = lax.axis_index("seq")
    mine = lax.axis_index("head")
    my_y, my_x = lax.div(me, side), lax.rem(me, side)

    def row_peer(step):
        return my_y * side + lax.rem(my_x + step, side)

    def column_peer(step):
        return lax.rem(my_y + step, tall) * side + my_x

    def head_peer(step):
        return lax.rem(mine + step, n_h)

    def remote(src, dst, send, recv, j, seq, head):
        return pltpu.make_async_remote_copy(
            src_ref=src,
            dst_ref=dst,
            send_sem=send.at[j],
            recv_sem=recv.at[j],
            device_id=(seq, head),
            device_id_type=MESH,
        )

    def to_row(buffer, send, recv):
        return lambda j: remote(
            buffer.at[0], buffer.at[j], send, recv, j, row_peer(j), mine
        )

    def to_column(buffer, send, recv):
        return lambda j: remote(
            buffer.at[0], buffer.at[j], send, recv, j, column_peer(j), mine
        )

    def to_heads(buffer, send, recv):
        return lambda j: remote(buffer.at[0], buffer.at[j], send, recv, j, me, head_peer(j))

    def back_row(source, target, send, recv):
        return lambda j: remote(
            source.at[j], target.at[j], send, recv, j, row_peer(side - j), mine
        )

    def back_column(source, target, send, recv):
        return lambda j: remote(
            source.at[j], target.at[j], send, recv, j, column_peer(tall - j), mine
        )

    barrier = pltpu.get_barrier_semaphore()

    def greet(seq, head):
        pl.semaphore_signal(barrier, inc=1, device_id=(seq, head), device_id_type=MESH)

    each(1, side, lambda j: greet(row_peer(j), mine))
    each(1, tall, lambda j: greet(column_peer(j), mine))
    each(1, n_h, lambda j: greet(me, head_peer(j)))

    loads = [
        pltpu.make_async_copy(src, dst, load.at[i])
        for i, (src, dst) in enumerate(
            (
                (q_hbm, q_raw),
                (k_hbm, k_raw),
                (do_hbm, d_out),
                (o_hbm, out),
                (qg_hbm, q_gain),
                (kg_hbm, k_gain),
                (v_hbm, values.at[0]),
                (order_hbm, order),
            )
        )
    ]
    for copy in loads:
        copy.start()

    squares_copy = to_heads(squares, sq_send, sq_recv)
    q_copy = to_row(q_in, qi_send, qi_recv)
    k_copy = to_column(k_in, ki_send, ki_recv)
    q_rows_copy = to_row(q_rows, qr_send, qr_recv)
    k_rows_copy = to_column(k_rows, kr_send, kr_recv)
    grads_copy = to_row(grads, gr_send, gr_recv)
    values_copy = to_column(values, va_send, va_recv)
    totals_copy = to_row(totals, to_send, to_recv)
    q_moment_copy = back_row(q_moment.at[0], q_moment.at[1], qm_send, qm_recv)
    k_moment_copy = back_column(k_moment.at[0], k_moment.at[1], km_send, km_recv)
    dq_copy = back_row(dq_out, dq_in, dq_send, dq_recv)
    dk_copy = back_column(dk_out, dk_in, dk_send, dk_recv)
    dv_copy = back_column(dv_out, dv_in, dv_send, dv_recv)
    inner_copy = to_heads(inner, inn_send, inn_recv)

    loads[0].wait()
    x = q_raw[...].astype(jnp.float32).T
    x_t[...] = x
    q_in[0] = x.astype(jnp.bfloat16)
    squares[0, 0:1] = jnp.sum(x * x, axis=0, keepdims=True)
    loads[1].wait()
    y = k_raw[...].astype(jnp.float32).T
    k_in[0] = y.astype(jnp.bfloat16)
    squares[0, 1:2] = jnp.sum(y * y, axis=0, keepdims=True)

    pl.semaphore_wait(barrier, side + tall + n_h - 3)
    each(1, n_h, lambda j: squares_copy(j).start())
    each(1, side, lambda j: q_copy(j).start())
    each(1, tall, lambda j: k_copy(j).start())

    loads[2].wait()
    loads[3].wait()
    grad = d_out[...].astype(jnp.float32)
    grads[0] = grad.T.astype(jnp.bfloat16)
    q_rows[0, 1:2] = jnp.sum((grad * out[...].astype(jnp.float32)).T, axis=0, keepdims=True)
    loads[4].wait()
    loads[5].wait()
    qg_t[...] = jnp.broadcast_to(q_gain[...].astype(jnp.float32), (rows, width)).T
    kg_t[...] = jnp.broadcast_to(k_gain[...].astype(jnp.float32), (rows, width)).T
    loads[6].wait()
    loads[7].wait()

    each(1, n_h, lambda j: squares_copy(j).wait_recv())
    rates = lax.rsqrt(jnp.sum(squares[...], axis=0) / features + EPSILON)
    q_rate, k_rate = rates[0:1], rates[1:2]
    q_rows[0, 0:1] = q_rate
    k_rows[0] = k_rate
    each(1, side, lambda j: q_rows_copy(j).start())
    each(1, tall, lambda j: k_rows_copy(j).start())
    each(1, side, lambda j: grads_copy(j).start())
    each(1, tall, lambda j: values_copy(j).start())

    def form_query(j):
        query = q_in[j].astype(jnp.float32) * q_rows[j, 0:1] * qg_t[...]
        queries[j] = query.astype(jnp.bfloat16)

    def form_keys(j):
        key = k_in[j].astype(jnp.float32) * k_rows[j] * kg_t[...]
        keys_t[j] = key.astype(jnp.bfloat16)
        keys[j] = key.T.astype(jnp.bfloat16)

    row_total = [0.0] * side

    def score_tile(jx, jy):
        query_group = order[row_peer(side - jx)]
        key_group = order[column_peer(tall - jy)]
        hidden = jnp.where(query_group >= key_group, 0.0, HIDDEN).astype(jnp.float32)
        score = dot(keys[jy], queries[jx], NN) * (root * LOG2E) + hidden
        scores[jx, jy] = score
        row_total[jx] += jnp.sum(jnp.exp2(score), axis=0, keepdims=True)

    form_query(0)
    form_keys(0)
    score_tile(0, 0)
    for jx in range(1, side):
        q_copy(jx).wait_recv()
        q_rows_copy(jx).wait_recv()
        form_query(jx)
        score_tile(jx, 0)
    for jy in range(1, tall):
        k_copy(jy).wait_recv()
        k_rows_copy(jy).wait_recv()
        form_keys(jy)
        for jx in range(side):
            score_tile(jx, jy)
    for jx in range(side):
        totals[0, lax.rem(my_x + side - jx, side)] = row_total[jx]
    each(1, side, lambda j: totals_copy(j).start())
    q_scale[...] = q_rate * qg_t[...]
    k_scale[...] = (k_rate * kg_t[...]).T
    each(1, side, lambda j: totals_copy(j).wait_recv())

    logs = [
        jnp.log2(sum(totals[i, lax.rem(my_x + side - jx, side)] for i in range(side)))
        for jx in range(side)
    ]
    ones = jnp.ones((16, rows), jnp.bfloat16)
    dq = [0.0] * side
    dk = [0.0] * tall
    dv = [0.0] * tall
    q_part = [0.0] * side
    k_part = [0.0] * tall

    def grad_tile(jx, jy):
        score = scores[jx, jy]
        probs = jnp.exp2(score - logs[jx])
        ds = probs * (dot(values[jy], grads[jx], NN) - q_rows[jx, 1:2])
        low = ds.astype(jnp.bfloat16)
        moment = ds * score
        q_part[jx] += jnp.sum(moment, axis=0, keepdims=True)
        k_part[jy] += dot(ones, moment.astype(jnp.bfloat16), NT)[0:1]
        dq[jx] += dot(keys_t[jy], low, NN)
        dk[jy] += dot(low, queries[jx], NT)
        dv[jy] += dot(probs.astype(jnp.bfloat16), grads[jx], NT)

    grad_tile(0, 0)
    for jx in range(1, side):
        grads_copy(jx).wait_recv()
    for jy in range(1, tall):
        values_copy(jy).wait_recv()
        for jx in range(side):
            grad_tile(jx, jy)
        k_moment[0, jy] = k_part[jy]
        k_moment_copy(jy).start()
        dk_out[jy] = (dk[jy] * root).astype(jnp.bfloat16)
        dk_copy(jy).start()
        dv_out[jy] = dv[jy].astype(jnp.bfloat16)
        dv_copy(jy).start()
    for jx in range(1, side):
        grad_tile(jx, 0)
        q_moment[0, jx] = q_part[jx]
        q_moment_copy(jx).start()
        dq_out[jx] = (dq[jx] * root).astype(jnp.bfloat16)
        dq_copy(jx).start()

    q_inner, k_inner = q_part[0], k_part[0]
    for jy in range(1, tall):
        k_moment_copy(jy).wait_recv()
        k_inner = k_inner + k_moment[1, jy]
    for jx in range(1, side):
        q_moment_copy(jx).wait_recv()
        q_inner = q_inner + q_moment[1, jx]
    inner[0, 0:1] = q_inner
    inner[0, 1:2] = k_inner
    each(1, n_h, lambda j: inner_copy(j).start())

    own_dq = dq[0] * root
    own_dk = dk[0] * root
    each(1, n_h, lambda j: inner_copy(j).wait_recv())
    products = jnp.sum(inner[...], axis=0) * (1.0 / (LOG2E * features))
    for jx in range(1, side):
        dq_copy(jx).wait_recv()
        own_dq = own_dq + dq_in[jx].astype(jnp.float32)
    grad_q = q_scale[...] * own_dq - x_t[...] * (q_rate * q_rate * products[0:1])
    d_q[...] = grad_q.T.astype(jnp.bfloat16)
    for jy in range(1, tall):
        dk_copy(jy).wait_recv()
        own_dk = own_dk + dk_in[jy].astype(jnp.float32)
    pull = jnp.broadcast_to(k_rate * k_rate * products[1:2], (width, rows)).T
    d_k[...] = (k_scale[...] * own_dk - k_raw[...].astype(jnp.float32) * pull).astype(jnp.bfloat16)
    own_dv = dv[0]
    for jy in range(1, tall):
        dv_copy(jy).wait_recv()
        own_dv = own_dv + dv_in[jy].astype(jnp.float32)
    d_v[...] = own_dv.astype(jnp.bfloat16)

    for copy in (squares_copy, inner_copy):
        each(1, n_h, lambda j: copy(j).wait_send())
    for copy in (q_copy, q_rows_copy, grads_copy, totals_copy, q_moment_copy, dq_copy):
        each(1, side, lambda j: copy(j).wait_send())
    for copy in (k_copy, k_rows_copy, values_copy, k_moment_copy, dk_copy, dv_copy):
        each(1, tall, lambda j: copy(j).wait_send())


def deliver(*refs):
    sems = refs[6]
    copies = [pltpu.make_async_copy(refs[i], refs[i + 3], sems.at[i]) for i in range(3)]
    for copy in copies:
        copy.start()
    for copy in copies:
        copy.wait()


def local(n_s, n_h, q_raw, k_raw, values, out, d_out, q_gain, k_gain, order):
    rows, width = q_raw.shape
    block = jax.ShapeDtypeStruct((rows, width), jnp.bfloat16)
    vmem = pl.BlockSpec(memory_space=pltpu.VMEM)
    hbm = pl.BlockSpec(memory_space=pltpu.HBM)
    low, wide = jnp.bfloat16, jnp.float32
    side, tall = grid_of(n_s)
    results = pl.pallas_call(
        functools.partial(kernel, n_s, n_h),
        out_shape=(block, block, block),
        in_specs=[hbm] * 8,
        out_specs=(vmem, vmem, vmem),
        scratch_shapes=[
            pltpu.SMEM((n_s,), jnp.int32),
            pltpu.VMEM((rows, width), low),
            pltpu.VMEM((rows, width), low),
            pltpu.VMEM((rows, width), low),
            pltpu.VMEM((rows, width), low),
            pltpu.VMEM((1, width), low),
            pltpu.VMEM((1, width), low),
            pltpu.VMEM((width, rows), wide),
            pltpu.VMEM((width, rows), wide),
            pltpu.VMEM((rows, width), wide),
            pltpu.VMEM((width, rows), wide),
            pltpu.VMEM((width, rows), wide),
            pltpu.VMEM((tall, rows, width), low),
            pltpu.VMEM((tall, width, rows), low),
            pltpu.VMEM((side, width, rows), low),
            pltpu.VMEM((side, tall, rows, rows), wide),
            pltpu.VMEM((n_h, 2, rows), wide),
            pltpu.VMEM((side, width, rows), low),
            pltpu.VMEM((tall, width, rows), low),
            pltpu.VMEM((side, 2, rows), wide),
            pltpu.VMEM((tall, 1, rows), wide),
            pltpu.VMEM((side, width, rows), low),
            pltpu.VMEM((tall, rows, width), low),
            pltpu.VMEM((side, side, 1, rows), wide),
            pltpu.VMEM((2, side, 1, rows), wide),
            pltpu.VMEM((2, tall, 1, rows), wide),
            pltpu.VMEM((side, width, rows), low),
            pltpu.VMEM((side, width, rows), low),
            pltpu.VMEM((tall, rows, width), low),
            pltpu.VMEM((tall, rows, width), low),
            pltpu.VMEM((tall, rows, width), low),
            pltpu.VMEM((tall, rows, width), low),
            pltpu.VMEM((n_h, 2, rows), wide),
            pltpu.SemaphoreType.DMA((8,)),
            pltpu.SemaphoreType.DMA((n_h,)),
            pltpu.SemaphoreType.DMA((n_h,)),
            pltpu.SemaphoreType.DMA((side,)),
            pltpu.SemaphoreType.DMA((side,)),
            pltpu.SemaphoreType.DMA((tall,)),
            pltpu.SemaphoreType.DMA((tall,)),
            pltpu.SemaphoreType.DMA((side,)),
            pltpu.SemaphoreType.DMA((side,)),
            pltpu.SemaphoreType.DMA((tall,)),
            pltpu.SemaphoreType.DMA((tall,)),
            pltpu.SemaphoreType.DMA((side,)),
            pltpu.SemaphoreType.DMA((side,)),
            pltpu.SemaphoreType.DMA((tall,)),
            pltpu.SemaphoreType.DMA((tall,)),
            pltpu.SemaphoreType.DMA((side,)),
            pltpu.SemaphoreType.DMA((side,)),
            pltpu.SemaphoreType.DMA((side,)),
            pltpu.SemaphoreType.DMA((side,)),
            pltpu.SemaphoreType.DMA((tall,)),
            pltpu.SemaphoreType.DMA((tall,)),
            pltpu.SemaphoreType.DMA((side,)),
            pltpu.SemaphoreType.DMA((side,)),
            pltpu.SemaphoreType.DMA((tall,)),
            pltpu.SemaphoreType.DMA((tall,)),
            pltpu.SemaphoreType.DMA((tall,)),
            pltpu.SemaphoreType.DMA((tall,)),
            pltpu.SemaphoreType.DMA((n_h,)),
            pltpu.SemaphoreType.DMA((n_h,)),
        ],
        compiler_params=pltpu.CompilerParams(
            collective_id=0, has_side_effects=True, vmem_limit_bytes=40 * 1024 * 1024
        ),
        cost_estimate=pl.CostEstimate(
            flops=10 * n_s * rows * rows * width,
            bytes_accessed=16 * rows * width,
            transcendentals=2 * n_s * rows * rows,
        ),
    )(
        *(
            pltpu.with_memory_space_constraint(array, pltpu.HBM)
            for array in (
                order,
                q_raw,
                k_raw,
                values,
                out,
                d_out,
                q_gain.reshape(1, width),
                k_gain.reshape(1, width),
            )
        )
    )
    return pl.pallas_call(
        deliver,
        out_shape=(block, block, block),
        in_specs=[vmem] * 3,
        out_specs=(hbm, hbm, hbm),
        scratch_shapes=[pltpu.SemaphoreType.DMA((3,))],
        compiler_params=pltpu.CompilerParams(vmem_limit_bytes=1024 * 1024),
    )(*(pltpu.with_memory_space_constraint(result, pltpu.VMEM) for result in results))


def solution(mesh):
    block = P("seq", "head")
    return jax.shard_map(
        functools.partial(local, mesh.shape["seq"], mesh.shape["head"]),
        mesh=mesh,
        in_specs=(block, block, block, block, block, P("head"), P("head"), P()),
        out_specs=(block, block, block),
        check_vma=False,
    )
```

time: 31.2 us -> 25.9 us (0.83)
  Pallas kernels: 28.5 us -> 25.1 us
  local copies, waits for them, and re-layouts: 1.89 us -> 0 us
    pallas_call x1, Pallas kernels: 26.8 us -> 24.3 us  [local(): pl.pallas_call(functools.partial(kernel, n_s, n_h), out_shape=(block, blo...]
    unnamed x6 -> x0, local copies, waits for them, and re-layouts: 1.89 us -> none
    pallas_call x1, Pallas kernels: 1.72 us -> 0.73 us  [local(): pl.pallas_call(deliver, out_shape=(block, block, block), in_specs=[vmem]...]
where the time goes in v3:
time: 25.9 us; the launch traced here: 25.7 us
  Pallas kernels  25.1 us (97%)
  between operations  0.64 us (2%)
    pallas_call x1, Pallas kernels, local(): pl.pallas_call(functools.partial(kernel, n_s, n_h), out_shape=(block, blo...  24.3 us
    pallas_call x1, Pallas kernels, local(): pl.pallas_call(deliver, out_shape=(block, block, block), in_specs=[vmem]...  0.73 us

profile of v3, /device:TPU:0, one launch (start us, length us, event | category | flops | bytes accessed | tf_op | source)
XLA Modules:
  0.0 25.7 jit_solution(13776785808622453300)
XLA Ops:
  0.6 24.3 %shard_map.103 = (bf16[384,128]{1,0:T(8,128)(2,1)S(1)}, bf16[384,128]{1,0:T(8,128)(2,1)S(1)}, bf16[384,128]{1,0:T(8,128)(2,1)S(1)}) custom-call(s32[4]{0:T(128)} %order_hbm.1, bf16[384,128]{1,0:T(8,128)(2,1)} %q_hbm.1, bf16[384,128]{1,0:T(8,128)(2,1)} %k_hbm.1, bf16[384,128]{1,0:T(8,128)(2,1)} %v_hbm.1, bf16[384,128]{1,0:T(8,128)(2,1)} %o_hbm.1, ...), custom_call_target="tpu_custom_call" | custom-call | flops 754974720 | bytes 786432 | tf_op jit(solution)/shard_map/pallas_call | solution.py:385
  25.0 0.7 %shard_map.104 = (bf16[384,128]{1,0:T(8,128)(2,1)}, bf16[384,128]{1,0:T(8,128)(2,1)}, bf16[384,128]{1,0:T(8,128)(2,1)}) custom-call(bf16[384,128]{1,0:T(8,128)(2,1)S(1)} %get-tuple-element.6.refs_0_, bf16[384,128]{1,0:T(8,128)(2,1)S(1)} %get-tuple-element.7.refs_1_, bf16[384,128]{1,0:T(8,128)(2,1)S(1)} %get-tuple-element.8.refs_2_), custom_call_target="tpu_custom_call" | custom-call | tf_op jit(solution)/shard_map/pallas_call | solution.py:477

commit v4 on v3

--- a/solution.py
+++ b/solution.py
@@ -68,6 +68,7 @@
     keys_t,
     queries,
     scores,
+    dprobs,
     squares,
     q_in,
     k_in,
@@ -255,13 +256,17 @@
 
     row_total = [0.0] * side
 
+    def seen(jx, jy):
+        return order[row_peer(side - jx)] >= order[column_peer(tall - jy)]
+
     def score_tile(jx, jy):
-        query_group = order[row_peer(side - jx)]
-        key_group = order[column_peer(tall - jy)]
-        hidden = jnp.where(query_group >= key_group, 0.0, HIDDEN).astype(jnp.float32)
-        score = dot(keys[jy], queries[jx], NN) * (root * LOG2E) + hidden
+        score = dot(keys[jy], queries[jx], NN) * (root * LOG2E)
         scores[jx, jy] = score
-        row_total[jx] += jnp.sum(jnp.exp2(score), axis=0, keepdims=True)
+        total = jnp.sum(jnp.exp2(score), axis=0, keepdims=True)
+        row_total[jx] += jnp.where(seen(jx, jy), total, 0.0)
+
+    def dprob_tile(jx, jy):
+        dprobs[jx, jy] = dot(values[jy], grads[jx], NN) - q_rows[jx, 1:2]
 
     form_query(0)
     form_keys(0)
@@ -280,8 +285,16 @@
     for jx in range(side):
         totals[0, lax.rem(my_x + side - jx, side)] = row_total[jx]
     each(1, side, lambda j: totals_copy(j).start())
+    dprob_tile(0, 0)
     q_scale[...] = q_rate * qg_t[...]
     k_scale[...] = (k_rate * kg_t[...]).T
+    for jx in range(1, side):
+        grads_copy(jx).wait_recv()
+        dprob_tile(jx, 0)
+    for jy in range(1, tall):
+        values_copy(jy).wait_recv()
+        for jx in range(side):
+            dprob_tile(jx, jy)
     each(1, side, lambda j: totals_copy(j).wait_recv())
 
     logs = [
@@ -295,37 +308,43 @@
     q_part = [0.0] * side
     k_part = [0.0] * tall
 
-    def grad_tile(jx, jy):
-        score = scores[jx, jy]
-        probs = jnp.exp2(score - logs[jx])
-        ds = probs * (dot(values[jy], grads[jx], NN) - q_rows[jx, 1:2])
-        low = ds.astype(jnp.bfloat16)
-        moment = ds * score
+    def probs_of(jx, jy):
+        return jnp.exp2(scores[jx, jy] - jnp.where(seen(jx, jy), logs[jx], -HIDDEN))
+
+    def ds_of(jx, jy, probs):
+        ds = probs * dprobs[jx, jy]
+        moment = ds * scores[jx, jy]
         q_part[jx] += jnp.sum(moment, axis=0, keepdims=True)
         k_part[jy] += dot(ones, moment.astype(jnp.bfloat16), NT)[0:1]
-        dq[jx] += dot(keys_t[jy], low, NN)
-        dk[jy] += dot(low, queries[jx], NT)
-        dv[jy] += dot(probs.astype(jnp.bfloat16), grads[jx], NT)
-
-    grad_tile(0, 0)
-    for jx in range(1, side):
-        grads_copy(jx).wait_recv()
+        return ds.astype(jnp.bfloat16)
+
     for jy in range(1, tall):
-        values_copy(jy).wait_recv()
+        probs = [probs_of(jx, jy) for jx in range(side)]
         for jx in range(side):
-            grad_tile(jx, jy)
-        k_moment[0, jy] = k_part[jy]
-        k_moment_copy(jy).start()
-        dk_out[jy] = (dk[jy] * root).astype(jnp.bfloat16)
-        dk_copy(jy).start()
+            dv[jy] += dot(probs[jx].astype(jnp.bfloat16), grads[jx], NT)
         dv_out[jy] = dv[jy].astype(jnp.bfloat16)
         dv_copy(jy).start()
+        lows = [ds_of(jx, jy, probs[jx]) for jx in range(side)]
+        for jx in range(side):
+            dk[jy] += dot(lows[jx], queries[jx], NT)
+        k_moment[0, jy] = k_part[jy]
+        dk_out[jy] = (dk[jy] * root).astype(jnp.bfloat16)
+        k_moment_copy(jy).start()
+        dk_copy(jy).start()
+        for jx in range(side):
+            dq[jx] += dot(keys_t[jy], lows[jx], NN)
     for jx in range(1, side):
-        grad_tile(jx, 0)
+        probs = probs_of(jx, 0)
+        low = ds_of(jx, 0, probs)
+        dq[jx] += dot(keys_t[0], low, NN)
         q_moment[0, jx] = q_part[jx]
+        dq_out[jx] = (dq[jx] * root).astype(jnp.bfloat16)
         q_moment_copy(jx).start()
-        dq_out[jx] = (dq[jx] * root).astype(jnp.bfloat16)
         dq_copy(jx).start()
+        dk[0] += dot(low, queries[jx], NT)
+        dv[0] += dot(probs.astype(jnp.bfloat16), grads[jx], NT)
+    probs = probs_of(0, 0)
+    low = ds_of(0, 0, probs)
 
     q_inner, k_inner = q_part[0], k_part[0]
     for jy in range(1, tall):
@@ -338,25 +357,26 @@
     inner[0, 1:2] = k_inner
     each(1, n_h, lambda j: inner_copy(j).start())
 
-    own_dq = dq[0] * root
-    own_dk = dk[0] * root
-    each(1, n_h, lambda j: inner_copy(j).wait_recv())
-    products = jnp.sum(inner[...], axis=0) * (1.0 / (LOG2E * features))
-    for jx in range(1, side):
-        dq_copy(jx).wait_recv()
-        own_dq = own_dq + dq_in[jx].astype(jnp.float32)
-    grad_q = q_scale[...] * own_dq - x_t[...] * (q_rate * q_rate * products[0:1])
-    d_q[...] = grad_q.T.astype(jnp.bfloat16)
-    for jy in range(1, tall):
-        dk_copy(jy).wait_recv()
-        own_dk = own_dk + dk_in[jy].astype(jnp.float32)
-    pull = jnp.broadcast_to(k_rate * k_rate * products[1:2], (width, rows)).T
-    d_k[...] = (k_scale[...] * own_dk - k_raw[...].astype(jnp.float32) * pull).astype(jnp.bfloat16)
-    own_dv = dv[0]
+    own_dv = dv[0] + dot(probs.astype(jnp.bfloat16), grads[0], NT)
+    own_dq = (dq[0] + dot(keys_t[0], low, NN)) * root
+    own_dk = (dk[0] + dot(low, queries[0], NT)) * root
     for jy in range(1, tall):
         dv_copy(jy).wait_recv()
         own_dv = own_dv + dv_in[jy].astype(jnp.float32)
     d_v[...] = own_dv.astype(jnp.bfloat16)
+    for jx in range(1, side):
+        dq_copy(jx).wait_recv()
+        own_dq = own_dq + dq_in[jx].astype(jnp.float32)
+    grad_q = q_scale[...] * own_dq
+    each(1, n_h, lambda j: inner_copy(j).wait_recv())
+    products = jnp.sum(inner[...], axis=0) * (1.0 / (LOG2E * features))
+    grad_q = grad_q - x_t[...] * (q_rate * q_rate * products[0:1])
+    d_q[...] = grad_q.T.astype(jnp.bfloat16)
+    pull = jnp.broadcast_to(k_rate * k_rate * products[1:2], (width, rows)).T
+    for jy in range(1, tall):
+        dk_copy(jy).wait_recv()
+        own_dk = own_dk + dk_in[jy].astype(jnp.float32)
+    d_k[...] = (k_scale[...] * own_dk - k_raw[...].astype(jnp.float32) * pull).astype(jnp.bfloat16)
 
     for copy in (squares_copy, inner_copy):
         each(1, n_h, lambda j: copy(j).wait_send())
@@ -404,6 +424,7 @@
             pltpu.VMEM((tall, width, rows), low),
             pltpu.VMEM((side, width, rows), low),
             pltpu.VMEM((side, tall, rows, rows), wide),
+            pltpu.VMEM((side, tall, rows, rows), wide),
             pltpu.VMEM((n_h, 2, rows), wide),
             pltpu.VMEM((side, width, rows), low),
             pltpu.VMEM((tall, width, rows), low),

time: 25.9 us -> 25.6 us (0.988)
  Pallas kernels: 25.1 us -> 24.8 us
where the time goes in v4:
time: 25.6 us; the launch traced here: 25.5 us
  Pallas kernels  24.8 us (97%)
  between operations  0.64 us (2%)
    pallas_call x1, Pallas kernels, local(): pl.pallas_call(functools.partial(kernel, n_s, n_h), out_shape=(block, blo...  24.1 us
    pallas_call x1, Pallas kernels, local(): pl.pallas_call(deliver, out_shape=(block, block, block), in_specs=[vmem]...  0.73 us

profile of v4, /device:TPU:0, one launch (start us, length us, event | category | flops | bytes accessed | tf_op | source)
XLA Modules:
  0.0 25.5 jit_solution(8625014066227522922)
XLA Ops:
  0.6 24.1 %shard_map.103 = (bf16[384,128]{1,0:T(8,128)(2,1)S(1)}, bf16[384,128]{1,0:T(8,128)(2,1)S(1)}, bf16[384,128]{1,0:T(8,128)(2,1)S(1)}) custom-call(s32[4]{0:T(128)} %order_hbm.1, bf16[384,128]{1,0:T(8,128)(2,1)} %q_hbm.1, bf16[384,128]{1,0:T(8,128)(2,1)} %k_hbm.1, bf16[384,128]{1,0:T(8,128)(2,1)} %v_hbm.1, bf16[384,128]{1,0:T(8,128)(2,1)} %o_hbm.1, ...), custom_call_target="tpu_custom_call" | custom-call | flops 754974720 | bytes 786432 | tf_op jit(solution)/shard_map/pallas_call | solution.py:405
  24.7 0.7 %shard_map.104 = (bf16[384,128]{1,0:T(8,128)(2,1)}, bf16[384,128]{1,0:T(8,128)(2,1)}, bf16[384,128]{1,0:T(8,128)(2,1)}) custom-call(bf16[384,128]{1,0:T(8,128)(2,1)S(1)} %get-tuple-element.6.refs_0_, bf16[384,128]{1,0:T(8,128)(2,1)S(1)} %get-tuple-element.7.refs_1_, bf16[384,128]{1,0:T(8,128)(2,1)S(1)} %get-tuple-element.8.refs_2_), custom_call_target="tpu_custom_call" | custom-call | tf_op jit(solution)/shard_map/pallas_call | solution.py:498

commit v5 on v4

--- a/solution.py
+++ b/solution.py
@@ -70,6 +70,10 @@
     scores,
     dprobs,
     squares,
+    up_in,
+    up_out,
+    down_in,
+    down_out,
     q_in,
     k_in,
     q_rows,
@@ -130,6 +134,9 @@
     def column_peer(step):
         return lax.rem(my_y + step, tall) * side + my_x
 
+    level, last = lax.div(mine, 2), n_h // 2 - 1
+    twin = level * 2 + 1 - lax.rem(mine, 2)
+
     def head_peer(step):
         return lax.rem(mine + step, n_h)
 
@@ -173,7 +180,16 @@
 
     each(1, side, lambda j: greet(row_peer(j), mine))
     each(1, tall, lambda j: greet(column_peer(j), mine))
-    each(1, n_h, lambda j: greet(me, head_peer(j)))
+    greet(me, twin)
+
+    @pl.when(level > 0)
+    def _():
+        greet(me, mine - 2)
+
+    @pl.when(level < last)
+    def _():
+        greet(me, mine + 2)
+
 
     loads = [
         pltpu.make_async_copy(src, dst, load.at[i])
@@ -193,7 +209,9 @@
     for copy in loads:
         copy.start()
 
-    squares_copy = to_heads(squares, sq_send, sq_recv)
+    twin_copy = remote(squares.at[0], squares.at[1], sq_send, sq_recv, 0, me, twin)
+    up_copy = remote(up_out, up_in, sq_send, sq_recv, 1, me, mine + 2)
+    down_copy = remote(down_out, down_in, sq_send, sq_recv, 2, me, mine - 2)
     q_copy = to_row(q_in, qi_send, qi_recv)
     k_copy = to_column(k_in, ki_send, ki_recv)
     q_rows_copy = to_row(q_rows, qr_send, qr_recv)
@@ -218,32 +236,63 @@
     k_in[0] = y.astype(jnp.bfloat16)
     squares[0, 1:2] = jnp.sum(y * y, axis=0, keepdims=True)
 
-    pl.semaphore_wait(barrier, side + tall + n_h - 3)
-    each(1, n_h, lambda j: squares_copy(j).start())
+    below = lax.div(level + last, last + 1)
+    above = lax.div(2 * last - level, last + 1)
+    pl.semaphore_wait(barrier, side + tall - 1 + below + above)
+
+    twin_copy.start()
     each(1, side, lambda j: q_copy(j).start())
     each(1, tall, lambda j: k_copy(j).start())
-
+    loads[6].wait()
+    each(1, tall, lambda j: values_copy(j).start())
     loads[2].wait()
-    loads[3].wait()
     grad = d_out[...].astype(jnp.float32)
     grads[0] = grad.T.astype(jnp.bfloat16)
+    each(1, side, lambda j: grads_copy(j).start())
+
+    loads[3].wait()
     q_rows[0, 1:2] = jnp.sum((grad * out[...].astype(jnp.float32)).T, axis=0, keepdims=True)
     loads[4].wait()
     loads[5].wait()
     qg_t[...] = jnp.broadcast_to(q_gain[...].astype(jnp.float32), (rows, width)).T
     kg_t[...] = jnp.broadcast_to(k_gain[...].astype(jnp.float32), (rows, width)).T
-    loads[6].wait()
     loads[7].wait()
 
-    each(1, n_h, lambda j: squares_copy(j).wait_recv())
-    rates = lax.rsqrt(jnp.sum(squares[...], axis=0) / features + EPSILON)
+    twin_copy.wait_recv()
+    pair = squares[0] + squares[1]
+
+    @pl.when(level == 0)
+    def _():
+        up_in[...] = jnp.zeros_like(up_in)
+
+    @pl.when(level > 0)
+    def _():
+        up_copy.wait_recv()
+
+    @pl.when(level < last)
+    def _():
+        up_out[...] = up_in[...] + pair
+        up_copy.start()
+
+    @pl.when(level == last)
+    def _():
+        down_in[...] = jnp.zeros_like(down_in)
+
+    @pl.when(level < last)
+    def _():
+        down_copy.wait_recv()
+
+    @pl.when(level > 0)
+    def _():
+        down_out[...] = down_in[...] + pair
+        down_copy.start()
+
+    rates = lax.rsqrt((pair + up_in[...] + down_in[...]) / features + EPSILON)
     q_rate, k_rate = rates[0:1], rates[1:2]
     q_rows[0, 0:1] = q_rate
     k_rows[0] = k_rate
     each(1, side, lambda j: q_rows_copy(j).start())
     each(1, tall, lambda j: k_rows_copy(j).start())
-    each(1, side, lambda j: grads_copy(j).start())
-    each(1, tall, lambda j: values_copy(j).start())
 
     def form_query(j):
         query = q_in[j].astype(jnp.float32) * q_rows[j, 0:1] * qg_t[...]
@@ -378,8 +427,17 @@
         own_dk = own_dk + dk_in[jy].astype(jnp.float32)
     d_k[...] = (k_scale[...] * own_dk - k_raw[...].astype(jnp.float32) * pull).astype(jnp.bfloat16)
 
-    for copy in (squares_copy, inner_copy):
-        each(1, n_h, lambda j: copy(j).wait_send())
+    twin_copy.wait_send()
+
+    @pl.when(level < last)
+    def _():
+        up_copy.wait_send()
+
+    @pl.when(level > 0)
+    def _():
+        down_copy.wait_send()
+
+    each(1, n_h, lambda j: inner_copy(j).wait_send())
     for copy in (q_copy, q_rows_copy, grads_copy, totals_copy, q_moment_copy, dq_copy):
         each(1, side, lambda j: copy(j).wait_send())
     for copy in (k_copy, k_rows_copy, values_copy, k_moment_copy, dk_copy, dv_copy):
@@ -425,7 +483,11 @@
             pltpu.VMEM((side, width, rows), low),
             pltpu.VMEM((side, tall, rows, rows), wide),
             pltpu.VMEM((side, tall, rows, rows), wide),
-            pltpu.VMEM((n_h, 2, rows), wide),
+            pltpu.VMEM((2, 2, rows), wide),
+            pltpu.VMEM((2, rows), wide),
+            pltpu.VMEM((2, rows), wide),
+            pltpu.VMEM((2, rows), wide),
+            pltpu.VMEM((2, rows), wide),
             pltpu.VMEM((side, width, rows), low),
             pltpu.VMEM((tall, width, rows), low),
             pltpu.VMEM((side, 2, rows), wide),
@@ -443,8 +505,8 @@
             pltpu.VMEM((tall, rows, width), low),
             pltpu.VMEM((n_h, 2, rows), wide),
             pltpu.SemaphoreType.DMA((8,)),
-            pltpu.SemaphoreType.DMA((n_h,)),
-            pltpu.SemaphoreType.DMA((n_h,)),
+            pltpu.SemaphoreType.DMA((3,)),
+            pltpu.SemaphoreType.DMA((3,)),
             pltpu.SemaphoreType.DMA((side,)),
             pltpu.SemaphoreType.DMA((side,)),
             pltpu.SemaphoreType.DMA((tall,)),

time: 25.6 us -> 33.1 us (1.29)
  Pallas kernels: 24.8 us -> 32.4 us
    pallas_call x1, Pallas kernels: 24.1 us -> 31.6 us  [local(): pl.pallas_call(functools.partial(kernel, n_s, n_h), out_shape=(block, blo...]
where the time goes in v5:
time: 33.1 us; the launch traced here: 33 us
  Pallas kernels  32.4 us (98%)
  between operations  0.64 us (2%)
    pallas_call x1, Pallas kernels, local(): pl.pallas_call(functools.partial(kernel, n_s, n_h), out_shape=(block, blo...  31.6 us
    pallas_call x1, Pallas kernels, local(): pl.pallas_call(deliver, out_shape=(block, block, block), in_specs=[vmem]...  0.73 us

profile of v5, /device:TPU:0, one launch (start us, length us, event | category | flops | bytes accessed | tf_op | source)
XLA Modules:
  0.0 33.0 jit_solution(12786572938117912612)
XLA Ops:
  0.6 31.6 %shard_map.103 = (bf16[384,128]{1,0:T(8,128)(2,1)S(1)}, bf16[384,128]{1,0:T(8,128)(2,1)S(1)}, bf16[384,128]{1,0:T(8,128)(2,1)S(1)}) custom-call(s32[4]{0:T(128)} %order_hbm.1, bf16[384,128]{1,0:T(8,128)(2,1)} %q_hbm.1, bf16[384,128]{1,0:T(8,128)(2,1)} %k_hbm.1, bf16[384,128]{1,0:T(8,128)(2,1)} %v_hbm.1, bf16[384,128]{1,0:T(8,128)(2,1)} %o_hbm.1, ...), custom_call_target="tpu_custom_call" | custom-call | flops 754974720 | bytes 786432 | tf_op jit(solution)/shard_map/pallas_call | solution.py:463
  32.3 0.7 %shard_map.104 = (bf16[384,128]{1,0:T(8,128)(2,1)}, bf16[384,128]{1,0:T(8,128)(2,1)}, bf16[384,128]{1,0:T(8,128)(2,1)}) custom-call(bf16[384,128]{1,0:T(8,128)(2,1)S(1)} %get-tuple-element.6.refs_0_, bf16[384,128]{1,0:T(8,128)(2,1)S(1)} %get-tuple-element.7.refs_1_, bf16[384,128]{1,0:T(8,128)(2,1)S(1)} %get-tuple-element.8.refs_2_), custom_call_target="tpu_custom_call" | custom-call | tf_op jit(solution)/shard_map/pallas_call | solution.py:560

commit v6 on v4

--- a/solution.py
+++ b/solution.py
@@ -318,33 +318,35 @@
         k_part[jy] += dot(ones, moment.astype(jnp.bfloat16), NT)[0:1]
         return ds.astype(jnp.bfloat16)
 
-    for jy in range(1, tall):
-        probs = [probs_of(jx, jy) for jx in range(side)]
+    probs, lows = {}, {}
+    tiles = [(jx, jy) for jy in range(tall) for jx in range(side)][1:]
+    for jx, jy in tiles:
+        probs[jx, jy] = probs_of(jx, jy)
+        lows[jx, jy] = ds_of(jx, jy, probs[jx, jy])
+        probs[jx, jy] = probs[jx, jy].astype(jnp.bfloat16)
+    for jy in range(1, tall):
+        k_moment[0, jy] = k_part[jy]
+        k_moment_copy(jy).start()
+    for jx in range(1, side):
+        q_moment[0, jx] = q_part[jx]
+        q_moment_copy(jx).start()
+    for jy in range(1, tall):
         for jx in range(side):
-            dv[jy] += dot(probs[jx].astype(jnp.bfloat16), grads[jx], NT)
+            dv[jy] += dot(probs[jx, jy], grads[jx], NT)
         dv_out[jy] = dv[jy].astype(jnp.bfloat16)
         dv_copy(jy).start()
-        lows = [ds_of(jx, jy, probs[jx]) for jx in range(side)]
+    for jx in range(1, side):
+        for jy in range(tall):
+            dq[jx] += dot(keys_t[jy], lows[jx, jy], NN)
+        dq_out[jx] = (dq[jx] * root).astype(jnp.bfloat16)
+        dq_copy(jx).start()
+    probs[0, 0] = probs_of(0, 0)
+    lows[0, 0] = ds_of(0, 0, probs[0, 0])
+    probs[0, 0] = probs[0, 0].astype(jnp.bfloat16)
+    for jy in range(1, tall):
         for jx in range(side):
-            dk[jy] += dot(lows[jx], queries[jx], NT)
-        k_moment[0, jy] = k_part[jy]
+            dk[jy] += dot(lows[jx, jy], queries[jx], NT)
         dk_out[jy] = (dk[jy] * root).astype(jnp.bfloat16)
-        k_moment_copy(jy).start()
-        dk_copy(jy).start()
-        for jx in range(side):
-            dq[jx] += dot(keys_t[jy], lows[jx], NN)
-    for jx in range(1, side):
-        probs = probs_of(jx, 0)
-        low = ds_of(jx, 0, probs)
-        dq[jx] += dot(keys_t[0], low, NN)
-        q_moment[0, jx] = q_part[jx]
-        dq_out[jx] = (dq[jx] * root).astype(jnp.bfloat16)
-        q_moment_copy(jx).start()
-        dq_copy(jx).start()
-        dk[0] += dot(low, queries[jx], NT)
-        dv[0] += dot(probs.astype(jnp.bfloat16), grads[jx], NT)
-    probs = probs_of(0, 0)
-    low = ds_of(0, 0, probs)
 
     q_inner, k_inner = q_part[0], k_part[0]
     for jy in range(1, tall):
@@ -356,10 +358,14 @@
     inner[0, 0:1] = q_inner
     inner[0, 1:2] = k_inner
     each(1, n_h, lambda j: inner_copy(j).start())
-
-    own_dv = dv[0] + dot(probs.astype(jnp.bfloat16), grads[0], NT)
-    own_dq = (dq[0] + dot(keys_t[0], low, NN)) * root
-    own_dk = (dk[0] + dot(low, queries[0], NT)) * root
+    each(1, tall, lambda j: dk_copy(j).start())
+
+    for jy in range(tall):
+        dq[0] += dot(keys_t[jy], lows[0, jy], NN)
+    for jx in range(side):
+        dk[0] += dot(lows[jx, 0], queries[jx], NT)
+        dv[0] += dot(probs[jx, 0], grads[jx], NT)
+    own_dv, own_dq, own_dk = dv[0], dq[0] * root, dk[0] * root
     for jy in range(1, tall):
         dv_copy(jy).wait_recv()
         own_dv = own_dv + dv_in[jy].astype(jnp.float32)

time: 25.6 us -> 24.4 us (0.953)
  Pallas kernels: 24.8 us -> 23.6 us
    pallas_call x1, Pallas kernels: 24.1 us -> 22.8 us  [local(): pl.pallas_call(functools.partial(kernel, n_s, n_h), out_shape=(block, blo...]
where the time goes in v6:
time: 24.4 us; the launch traced here: 24.2 us
  Pallas kernels  23.6 us (97%)
  between operations  0.64 us (3%)
    pallas_call x1, Pallas kernels, local(): pl.pallas_call(functools.partial(kernel, n_s, n_h), out_shape=(block, blo...  22.8 us
    pallas_call x1, Pallas kernels, local(): pl.pallas_call(deliver, out_shape=(block, block, block), in_specs=[vmem]...  0.73 us

profile of v6, /device:TPU:0, one launch (start us, length us, event | category | flops | bytes accessed | tf_op | source)
XLA Modules:
  0.0 24.2 jit_solution(154715185866035296)
XLA Ops:
  0.6 22.8 %shard_map.103 = (bf16[384,128]{1,0:T(8,128)(2,1)S(1)}, bf16[384,128]{1,0:T(8,128)(2,1)S(1)}, bf16[384,128]{1,0:T(8,128)(2,1)S(1)}) custom-call(s32[4]{0:T(128)} %order_hbm.1, bf16[384,128]{1,0:T(8,128)(2,1)} %q_hbm.1, bf16[384,128]{1,0:T(8,128)(2,1)} %k_hbm.1, bf16[384,128]{1,0:T(8,128)(2,1)} %v_hbm.1, bf16[384,128]{1,0:T(8,128)(2,1)} %o_hbm.1, ...), custom_call_target="tpu_custom_call" | custom-call | flops 754974720 | bytes 786432 | tf_op jit(solution)/shard_map/pallas_call | solution.py:411
  23.5 0.7 %shard_map.104 = (bf16[384,128]{1,0:T(8,128)(2,1)}, bf16[384,128]{1,0:T(8,128)(2,1)}, bf16[384,128]{1,0:T(8,128)(2,1)}) custom-call(bf16[384,128]{1,0:T(8,128)(2,1)S(1)} %get-tuple-element.6.refs_0_, bf16[384,128]{1,0:T(8,128)(2,1)S(1)} %get-tuple-element.7.refs_1_, bf16[384,128]{1,0:T(8,128)(2,1)S(1)} %get-tuple-element.8.refs_2_), custom_call_target="tpu_custom_call" | custom-call | tf_op jit(solution)/shard_map/pallas_call | solution.py:504

commit v7 on v6

--- a/solution.py
+++ b/solution.py
@@ -208,6 +208,17 @@
     dv_copy = back_column(dv_out, dv_in, dv_send, dv_recv)
     inner_copy = to_heads(inner, inn_send, inn_recv)
 
+    def alternate(along_row, along_column):
+        @pl.when(lax.rem(mine, 2) == 0)
+        def _():
+            each(1, side, lambda j: along_row(j).start())
+            each(1, tall, lambda j: along_column(j).start())
+
+        @pl.when(lax.rem(mine, 2) == 1)
+        def _():
+            each(1, tall, lambda j: along_column(j).start())
+            each(1, side, lambda j: along_row(j).start())
+
     loads[0].wait()
     x = q_raw[...].astype(jnp.float32).T
     x_t[...] = x
@@ -220,8 +231,7 @@
 
     pl.semaphore_wait(barrier, side + tall + n_h - 3)
     each(1, n_h, lambda j: squares_copy(j).start())
-    each(1, side, lambda j: q_copy(j).start())
-    each(1, tall, lambda j: k_copy(j).start())
+    alternate(q_copy, k_copy)
 
     loads[2].wait()
     loads[3].wait()
@@ -242,8 +252,7 @@
     k_rows[0] = k_rate
     each(1, side, lambda j: q_rows_copy(j).start())
     each(1, tall, lambda j: k_rows_copy(j).start())
-    each(1, side, lambda j: grads_copy(j).start())
-    each(1, tall, lambda j: values_copy(j).start())
+    alternate(grads_copy, values_copy)
 
     def form_query(j):
         query = q_in[j].astype(jnp.float32) * q_rows[j, 0:1] * qg_t[...]
@@ -334,12 +343,11 @@
         for jx in range(side):
             dv[jy] += dot(probs[jx, jy], grads[jx], NT)
         dv_out[jy] = dv[jy].astype(jnp.bfloat16)
-        dv_copy(jy).start()
     for jx in range(1, side):
         for jy in range(tall):
             dq[jx] += dot(keys_t[jy], lows[jx, jy], NN)
         dq_out[jx] = (dq[jx] * root).astype(jnp.bfloat16)
-        dq_copy(jx).start()
+    alternate(dq_copy, dv_copy)
     probs[0, 0] = probs_of(0, 0)
     lows[0, 0] = ds_of(0, 0, probs[0, 0])
     probs[0, 0] = probs[0, 0].astype(jnp.bfloat16)
@@ -479,7 +487,7 @@
             pltpu.SemaphoreType.DMA((n_h,)),
         ],
         compiler_params=pltpu.CompilerParams(
-            collective_id=0, has_side_effects=True, vmem_limit_bytes=40 * 1024 * 1024
+            collective_id=0, has_side_effects=True, vmem_limit_bytes=56 * 1024 * 1024
         ),
         cost_estimate=pl.CostEstimate(
             flops=10 * n_s * rows * rows * width,

time: 24.4 us -> 27.7 us (1.14)
  local copies, waits for them, and re-layouts: 0 us -> 2.67 us
  Pallas kernels: 23.6 us -> 24.2 us
    unnamed x0 -> x6, local copies, waits for them, and re-layouts: none -> 2.67 us
    pallas_call x1, Pallas kernels: 22.8 us -> 23.5 us  [local(): pl.pallas_call(functools.partial(kernel, n_s, n_h), out_shape=(block, blo...]
where the time goes in v7:
time: 27.7 us; the launch traced here: 27.5 us
  Pallas kernels  24.2 us (87%)
  local copies, waits for them, and re-layouts  2.67 us (10%)
  between operations  0.65 us (2%)
    pallas_call x1, Pallas kernels, local(): pl.pallas_call(functools.partial(kernel, n_s, n_h), out_shape=(block, blo...  23.5 us
    unnamed x6, local copies, waits for them, and re-layouts  2.67 us
    pallas_call x1, Pallas kernels, local(): pl.pallas_call(deliver, out_shape=(block, block, block), in_specs=[vmem]...  0.73 us

profile of v7, /device:TPU:0, one launch (start us, length us, event | category | flops | bytes accessed | tf_op | source)
XLA Modules:
  0.0 27.5 jit_solution(10346791248594339138)
XLA Ops:
  0.6 23.5 %shard_map.103 = (bf16[384,128]{1,0:T(8,128)(2,1)}, bf16[384,128]{1,0:T(8,128)(2,1)}, bf16[384,128]{1,0:T(8,128)(2,1)}) custom-call(s32[4]{0:T(128)} %order_hbm.1, bf16[384,128]{1,0:T(8,128)(2,1)} %q_hbm.1, bf16[384,128]{1,0:T(8,128)(2,1)} %k_hbm.1, bf16[384,128]{1,0:T(8,128)(2,1)} %v_hbm.1, bf16[384,128]{1,0:T(8,128)(2,1)} %o_hbm.1, ...), custom_call_target="tpu_custom_call" | custom-call | flops 754974720 | bytes 786432 | tf_op jit(solution)/shard_map/pallas_call | solution.py:419
  24.1 0.0 copy-start
  24.1 0.9 %copy-done = bf16[384,128]{1,0:T(8,128)(2,1)S(1)} copy-done((bf16[384,128]{1,0:T(8,128)(2,1)S(1)}, bf16[384,128]{1,0:T(8,128)(2,1)}, u32[]{:S(2)}) %copy-start) | copy-done | bytes 98328
  25.0 0.0 copy-start.1
  25.0 0.9 %copy-done.1 = bf16[384,128]{1,0:T(8,128)(2,1)S(1)} copy-done((bf16[384,128]{1,0:T(8,128)(2,1)S(1)}, bf16[384,128]{1,0:T(8,128)(2,1)}, u32[]{:S(2)}) %copy-start.1) | copy-done | bytes 98328
  25.9 0.0 copy-start.2
  25.9 0.9 %copy-done.2 = bf16[384,128]{1,0:T(8,128)(2,1)S(1)} copy-done((bf16[384,128]{1,0:T(8,128)(2,1)S(1)}, bf16[384,128]{1,0:T(8,128)(2,1)}, u32[]{:S(2)}) %copy-start.2) | copy-done | bytes 98328
  26.8 0.7 %shard_map.104 = (bf16[384,128]{1,0:T(8,128)(2,1)}, bf16[384,128]{1,0:T(8,128)(2,1)}, bf16[384,128]{1,0:T(8,128)(2,1)}) custom-call(bf16[384,128]{1,0:T(8,128)(2,1)S(1)} %copy-done, bf16[384,128]{1,0:T(8,128)(2,1)S(1)} %copy-done.1, bf16[384,128]{1,0:T(8,128)(2,1)S(1)} %copy-done.2), custom_call_target="tpu_custom_call" | custom-call | tf_op jit(solution)/shard_map/pallas_call | solution.py:512
Async XLA Ops:
  24.1 0.9 %copy-start = (bf16[384,128]{1,0:T(8,128)(2,1)S(1)}, bf16[384,128]{1,0:T(8,128)(2,1)}, u32[]{:S(2)}) copy-start(bf16[384,128]{1,0:T(8,128)(2,1)} %get-tuple-element.6.refs_0_) | copy-start | bytes 294916
  25.0 0.9 %copy-start.1 = (bf16[384,128]{1,0:T(8,128)(2,1)S(1)}, bf16[384,128]{1,0:T(8,128)(2,1)}, u32[]{:S(2)}) copy-start(bf16[384,128]{1,0:T(8,128)(2,1)} %get-tuple-element.7.refs_1_) | copy-start | bytes 294916
  25.9 0.9 %copy-start.2 = (bf16[384,128]{1,0:T(8,128)(2,1)S(1)}, bf16[384,128]{1,0:T(8,128)(2,1)}, u32[]{:S(2)}) copy-start(bf16[384,128]{1,0:T(8,128)(2,1)} %get-tuple-element.8.refs_2_) | copy-start | bytes 294916

commit v8 on v7

--- a/solution.py
+++ b/solution.py
@@ -487,7 +487,7 @@
             pltpu.SemaphoreType.DMA((n_h,)),
         ],
         compiler_params=pltpu.CompilerParams(
-            collective_id=0, has_side_effects=True, vmem_limit_bytes=56 * 1024 * 1024
+            collective_id=0, has_side_effects=True, vmem_limit_bytes=43 * 1024 * 1024
         ),
         cost_estimate=pl.CostEstimate(
             flops=10 * n_s * rows * rows * width,

time: 27.7 us -> 24.3 us (0.88)
  local copies, waits for them, and re-layouts: 2.67 us -> 0 us
  Pallas kernels: 24.2 us -> 23.5 us
    unnamed x6 -> x0, local copies, waits for them, and re-layouts: 2.67 us -> none
    pallas_call x1, Pallas kernels: 23.5 us -> 22.7 us  [local(): pl.pallas_call(functools.partial(kernel, n_s, n_h), out_shape=(block, blo...]
where the time goes in v8:
time: 24.3 us; the launch traced here: 24.1 us
  Pallas kernels  23.5 us (97%)
  between operations  0.64 us (3%)
    pallas_call x1, Pallas kernels, local(): pl.pallas_call(functools.partial(kernel, n_s, n_h), out_shape=(block, blo...  22.7 us
    pallas_call x1, Pallas kernels, local(): pl.pallas_call(deliver, out_shape=(block, block, block), in_specs=[vmem]...  0.73 us

profile of v8, /device:TPU:0, one launch (start us, length us, event | category | flops | bytes accessed | tf_op | source)
XLA Modules:
  0.0 24.1 jit_solution(11157073621077889164)
XLA Ops:
  0.6 22.7 %shard_map.103 = (bf16[384,128]{1,0:T(8,128)(2,1)S(1)}, bf16[384,128]{1,0:T(8,128)(2,1)S(1)}, bf16[384,128]{1,0:T(8,128)(2,1)S(1)}) custom-call(s32[4]{0:T(128)} %order_hbm.1, bf16[384,128]{1,0:T(8,128)(2,1)} %q_hbm.1, bf16[384,128]{1,0:T(8,128)(2,1)} %k_hbm.1, bf16[384,128]{1,0:T(8,128)(2,1)} %v_hbm.1, bf16[384,128]{1,0:T(8,128)(2,1)} %o_hbm.1, ...), custom_call_target="tpu_custom_call" | custom-call | flops 754974720 | bytes 786432 | tf_op jit(solution)/shard_map/pallas_call | solution.py:419
  23.4 0.7 %shard_map.104 = (bf16[384,128]{1,0:T(8,128)(2,1)}, bf16[384,128]{1,0:T(8,128)(2,1)}, bf16[384,128]{1,0:T(8,128)(2,1)}) custom-call(bf16[384,128]{1,0:T(8,128)(2,1)S(1)} %get-tuple-element.6.refs_0_, bf16[384,128]{1,0:T(8,128)(2,1)S(1)} %get-tuple-element.7.refs_1_, bf16[384,128]{1,0:T(8,128)(2,1)S(1)} %get-tuple-element.8.refs_2_), custom_call_target="tpu_custom_call" | custom-call | tf_op jit(solution)/shard_map/pallas_call | solution.py:512
